TPU v7x, 128 devices: a whole 4x4x4 slice. The times are simulated.
128 devices in a mesh: row: 8 (over y, core), col: 16 (over x, z).
Axes of the slice: x: 4, y: 4, z: 4, core: 2. Of those that a mesh axis runs over, the one named last changes fastest.
Arguments:
- inputs: bfloat16 [2048, 8192], P('col', 'row'), may hold values from -6 to 6
- grad_out: bfloat16 [2048, 8192], P('col', 'row'), may hold values from -0.59765625 to 0.59765625
- gate_pre: bfloat16 [2048, 14336], P('row', 'col'), may hold values from -9 to 9
- up_pre: bfloat16 [2048, 14336], P('row', 'col'), may hold values from -6 to 6
- w_gate: bfloat16 [8192, 14336], P('row', 'col'), may hold values from -0.125 to 0.125
- w_up: bfloat16 [8192, 14336], P('row', 'col'), may hold values from -0.125 to 0.125
- w_down: bfloat16 [14336, 8192], P('col', 'row'), may hold values from -0.09375 to 0.09375
- mask_gate: int32 [64, 112], P('row', 'col'), may hold values 0 or 1
- mask_up: int32 [64, 112], P('row', 'col'), may hold values 0 or 1
- mask_down: int32 [112, 64], P('col', 'row'), may hold values 0 or 1
Outputs:
- grad_inputs: bfloat16 [2048, 8192], P('col', 'row')
- grad_gate: bfloat16 [8192, 14336], P('row', 'col')
- grad_up: bfloat16 [8192, 14336], P('row', 'col')
- grad_down: bfloat16 [14336, 8192], P('col', 'row')
All inputs are finite; a program needn't handle non-finite values. No bound on the sum of `mask_gate` or of `mask_up` or of `mask_down` on one device may be relied on, other than what follows from the above.
Results may differ from a plain program's by a relative error of at most 0.005.
Values may be sent and summed in bfloat16 or wider, within the bound.
A program may use at most 128 MiB of HBM per device.

v0:
```python
import jax
import jax.numpy as jnp
from jax import lax
from jax.sharding import PartitionSpec as P


def expand(mask, block):
    return jnp.repeat(jnp.repeat(mask, block, 0), block, 1).astype(jnp.bfloat16)


def swiglu_grads(hidden_grad, gate_pre, up_pre):
    gated = gate_pre.astype(jnp.float32)
    upper = up_pre.astype(jnp.float32)
    sigma = jax.nn.sigmoid(gated)
    act = (gated * sigma * upper).astype(jnp.bfloat16)
    grad_g = (hidden_grad * upper * sigma * (1.0 + gated * (1.0 - sigma))).astype(jnp.bfloat16)
    grad_u = (hidden_grad * gated * sigma).astype(jnp.bfloat16)
    return (act, grad_g, grad_u)


def per_device(
    inputs, grad_out, gate_pre, up_pre, w_gate, w_up, w_down, mask_gate, mask_up, mask_down
):
    block = w_gate.shape[0] // mask_gate.shape[0]
    keep_gate = expand(mask_gate, block)
    keep_up = expand(mask_up, block)
    keep_down = expand(mask_down, block)
    gate_eff = w_gate * keep_gate
    up_eff = w_up * keep_up
    down_eff = w_down * keep_down
    contract = (((1,), (1,)), ((), ()))
    tokens_dim = (((0,), (0,)), ((), ()))
    grad_all = lax.all_gather(grad_out, "col", axis=0, tiled=True)
    hidden_grad = lax.psum_scatter(
        lax.dot_general(grad_all, down_eff, contract, preferred_element_type=jnp.float32),
        "row",
        scatter_dimension=0,
        tiled=True,
    )
    act, grad_g, grad_u = swiglu_grads(hidden_grad, gate_pre, up_pre)
    act_all, grad_g_all, grad_u_all = (
        lax.all_gather(act, "row", axis=0, tiled=True),
        lax.all_gather(grad_g, "row", axis=0, tiled=True),
        lax.all_gather(grad_u, "row", axis=0, tiled=True),
    )
    first = lax.dot_general(grad_g_all, gate_eff, contract, preferred_element_type=jnp.float32)
    grad_inputs = lax.psum_scatter(
        first + lax.dot_general(grad_u_all, up_eff, contract, preferred_element_type=jnp.float32),
        "col",
        scatter_dimension=0,
        tiled=True,
    ).astype(jnp.bfloat16)
    grad_down = lax.dot_general(act_all, grad_all, tokens_dim, preferred_element_type=jnp.float32)
    grad_down = (grad_down * keep_down.astype(jnp.float32)).astype(jnp.bfloat16)
    input_all = lax.all_gather(inputs, "col", axis=0, tiled=True)
    grad_gate = lax.dot_general(
        input_all, grad_g_all, tokens_dim, preferred_element_type=jnp.float32
    )
    grad_gate = (grad_gate * keep_gate.astype(jnp.float32)).astype(jnp.bfloat16)
    grad_up = lax.dot_general(input_all, grad_u_all, tokens_dim, preferred_element_type=jnp.float32)
    grad_up = (grad_up * keep_up.astype(jnp.float32)).astype(jnp.bfloat16)
    return (grad_inputs, grad_gate, grad_up, grad_down)


def solution(mesh):
    placed = (
        P("col", "row"),
        P("col", "row"),
        P("row", "col"),
        P("row", "col"),
        P("row", "col"),
        P("row", "col"),
        P("col", "row"),
        P("row", "col"),
        P("row", "col"),
        P("col", "row"),
    )
    return jax.shard_map(
        per_device,
        mesh=mesh,
        in_specs=placed,
        out_specs=(P("col", "row"), P("row", "col"), P("row", "col"), P("col", "row")),
        check_vma=False,
    )
```

profile of v0, /device:TPU:1, one launch (start us, length us, event | category | flops | bytes accessed | tf_op | source)
XLA Modules:
  0.0 384.1 jit_solution(13315913721828843192)
XLA Ops:
  7.2 0.0 all-gather.6.cloned.1.call-start
  7.2 0.7 all-gather.6.cloned.1.call-update
  7.9 0.0 reduce-scatter.3.cloned.1.call-start
  7.9 0.7 convert_element_type.69
  8.6 56.4 %all-gather.6.cloned.1.call-done = bf16[2048,1024]{1,0:T(8,128)(2,1)} async-done(((bf16[128,1024]{1,0:T(8,128)(2,1)}), bf16[2048,1024]{1,0:T(8,128)(2,1)}) %all-gather.6.cloned.1.call-update) | async-done | bytes 4194320 | tf_op jit(solution)/shard_map/all_gather | solution.py:33
  65.1 1.1 broadcast_in_dim.19
  66.2 0.0 copy-start.1
  66.2 1.3 copy-done.1
  67.5 9.7 %convolution_bitcast_fusion = f32[2048,896]{0,1:T(8,128)} fusion(bf16[2048,1024]{1,0:T(8,128)(2,1)} %all-gather.6.cloned.1.call-done, bf16[896,1024]{1,0:T(8,128)(2,1)} %param.16, bf16[112,8,8,128]{3,2,1,0:T(8,128)(2,1)S(1)} %bitcast.47), kind=kOutput, calls=%fused_computation | convolution fusion | flops 3759013888 | bytes 15204352 | tf_op jit(solution)/shard_map/dot_general | solution.py:35
  77.2 0.0 copy-start.2
  77.2 0.0 copy-start.3
  77.2 0.0 reduce-scatter.3.cloned.1.call-update
  77.2 0.0 copy-start.4
  77.2 0.0 all-gather.8.cloned.1.call-start
  77.3 0.9 copy-done.2
  78.2 0.2 copy.14
  78.4 0.0 copy-done.3
  78.4 0.2 copy.15
  78.6 0.0 copy-start.5
  78.6 45.2 %reduce-scatter.3.cloned.1.call-done = f32[256,896]{0,1:T(8,128)} async-done(((f32[2048,896]{0,1:T(8,128)}), f32[256,896]{0,1:T(8,128)}) %reduce-scatter.3.cloned.1.call-update) | async-done | bytes 917520 | tf_op jit(solution)/shard_map/reduce_scatter | solution.py:34
  123.8 2.8 fusion.12
  126.6 0.0 all-gather.8.cloned.1.call-update
  126.6 0.0 all-gather.10.cloned.1.call-start
  126.7 0.5 all-gather.10.cloned.1.call-update
  127.2 0.0 all-gather.12.cloned.1.call-start
  127.3 0.5 all-gather.12.cloned.1.call-update
  127.8 0.0 all-gather.14.cloned.1.call-start
  127.8 0.5 all-gather.14.cloned.1.call-update
  128.4 0.2 reduce-scatter.5.cloned.1.call-start
  128.6 0.0 copy-done.4
  128.6 0.1 copy.16
  128.7 0.1 broadcast_bitcast_fusion.1
  128.8 2.9 copy.17
  131.7 0.0 copy-done.5
  131.7 0.1 copy.18
  131.8 0.1 broadcast_bitcast_fusion
  131.9 3.8 copy.19
  135.7 0.0 copy-start
  135.7 1.4 bitcast_multiply_fusion.3
  137.1 0.9 copy-done
  137.9 0.1 bitcast_multiply_fusion.2
  138.0 23.2 %all-gather.8.cloned.1.call-done = bf16[2048,896]{0,1:T(8,128)(2,1)} async-done(((bf16[256,896]{0,1:T(8,128)(2,1)}), bf16[2048,896]{0,1:T(8,128)(2,1)}) %all-gather.8.cloned.1.call-update) | async-done | bytes 3670032 | tf_op jit(solution)/shard_map/all_gather | solution.py:43
  161.2 10.4 %fusion.13 = f32[2048,1024]{1,0:T(8,128)} fusion(bf16[2048,896]{0,1:T(8,128)(2,1)} %all-gather.8.cloned.1.call-done, bf16[1024,896]{0,1:T(8,128)(2,1)} %bitcast_multiply_fusion.3), kind=kOutput, calls=%fused_computation.31 | convolution fusion | flops 3758096384 | bytes 13893632 | tf_op jit(solution)/shard_map/dot_general | solution.py:46
  171.7 26.5 %all-gather.10.cloned.1.call-done = bf16[2048,896]{0,1:T(8,128)(2,1)} async-done(((bf16[256,896]{0,1:T(8,128)(2,1)}), bf16[2048,896]{0,1:T(8,128)(2,1)}) %all-gather.10.cloned.1.call-update) | async-done | bytes 3670032 | tf_op jit(solution)/shard_map/all_gather | solution.py:44
  198.2 10.2 %convolution_add_fusion = f32[2048,1024]{1,0:T(8,128)} fusion(f32[2048,1024]{1,0:T(8,128)} %fusion.13, bf16[2048,896]{0,1:T(8,128)(2,1)} %all-gather.10.cloned.1.call-done, bf16[1024,896]{0,1:T(8,128)(2,1)S(1)} %bitcast_multiply_fusion.2), kind=kOutput, calls=%fused_computation.1 | convolution fusion | flops 3760193536 | bytes 22282240 | tf_op jit(solution)/shard_map/dot_general | solution.py:48
  208.4 0.0 reduce-scatter.5.cloned.1.call-update
  208.4 44.0 %all-gather.12.cloned.1.call-done = bf16[2048,1024]{1,0:T(8,128)(2,1)} async-done(((bf16[128,1024]{1,0:T(8,128)(2,1)}), bf16[2048,1024]{1,0:T(8,128)(2,1)}) %all-gather.12.cloned.1.call-update) | async-done | bytes 4194320 | tf_op jit(solution)/shard_map/all_gather | solution.py:55
  252.4 7.3 %fusion.1 = bf16[1024,896]{0,1:T(8,128)(2,1)S(1)} fusion(bf16[2048,896]{0,1:T(8,128)(2,1)} %all-gather.8.cloned.1.call-done, bf16[2048,1024]{1,0:T(8,128)(2,1)} %all-gather.12.cloned.1.call-done, bf16[1024,7]{0,1:T(8,128)(2,1)S(1)} %bitcast.51), kind=kOutput, calls=%fused_computation.5 | convolution fusion | flops 3760848896 | bytes 9713664 | tf_op jit(solution)/shard_map/dot_general | solution.py:56
  259.7 2.5 copy.20
  262.1 7.7 %fusion = bf16[1024,896]{0,1:T(8,128)(2,1)S(1)} fusion(bf16[2048,896]{0,1:T(8,128)(2,1)} %all-gather.10.cloned.1.call-done, bf16[2048,1024]{1,0:T(8,128)(2,1)} %all-gather.12.cloned.1.call-done, bf16[1024,7]{0,1:T(8,128)(2,1)S(1)} %bitcast.53), kind=kOutput, calls=%fused_computation.3 | convolution fusion | flops 3760848896 | bytes 9713664 | tf_op jit(solution)/shard_map/dot_general | solution.py:60
  269.8 2.5 copy.21
  272.3 15.6 %all-gather.14.cloned.1.call-done = bf16[2048,896]{0,1:T(8,128)(2,1)} async-done(((bf16[256,896]{0,1:T(8,128)(2,1)}), bf16[2048,896]{0,1:T(8,128)(2,1)}) %all-gather.14.cloned.1.call-update) | async-done | bytes 3670032 | tf_op jit(solution)/shard_map/all_gather | solution.py:42
  287.8 9.0 %multiply_convert_fusion = bf16[896,1024]{1,0:T(8,128)(2,1)} fusion(bf16[2048,896]{0,1:T(8,128)(2,1)} %all-gather.14.cloned.1.call-done, bf16[2048,1024]{1,0:T(8,128)(2,1)} %all-gather.6.cloned.1.call-done, bf16[112,8,8,128]{3,2,1,0:T(8,128)(2,1)} %bitcast.48), kind=kOutput, calls=%fused_computation.6 | convolution fusion | flops 3760848896 | bytes 11534336 | tf_op jit(solution)/shard_map/dot_general | solution.py:53
  296.8 78.6 %reduce-scatter.5.cloned.1.call-done = f32[128,1024]{1,0:T(8,128)} async-done(((f32[2048,1024]{1,0:T(8,128)}), f32[128,1024]{1,0:T(8,128)}) %reduce-scatter.5.cloned.1.call-update) | async-done | bytes 524304 | tf_op jit(solution)/shard_map/reduce_scatter | solution.py:47
  375.5 1.8 convert_element_type.82
  (5 shorter events, 0.1 us)
Async XLA Ops:
  7.2 57.9 %all-gather.6.cloned.1.call-start = ((), (), s32[]{:S(2)}) async-start(), calls=%async_computation.2 | async-start | bytes 4456448 | tf_op jit(solution)/shard_map/all_gather | solution.py:33
  7.9 115.9 %reduce-scatter.3.cloned.1.call-start = ((), (), s32[]{:S(2)}) async-start(), calls=%async_computation.3 | async-start | bytes 8257536 | tf_op jit(solution)/shard_map/reduce_scatter | solution.py:34
  66.2 1.3 copy-start.1
  77.2 1.0 copy-start.2
  77.2 1.2 copy-start.3
  77.2 51.4 %copy-start.4 = (s32[8,7]{1,0:T(8,128)S(1)}, s32[8,7]{1,0:T(8,128)}, u32[]{:S(2)}) copy-start(s32[8,7]{1,0:T(8,128)} %param.17) | copy-start | bytes 676
  77.2 84.0 %all-gather.8.cloned.1.call-start = ((), (), s32[]{:S(2)}) async-start(), calls=%async_computation.4 | async-start | bytes 4128768 | tf_op jit(solution)/shard_map/all_gather | solution.py:43
  78.6 53.1 %copy-start.5 = (s32[8,7]{1,0:T(8,128)S(1)}, s32[8,7]{1,0:T(8,128)}, u32[]{:S(2)}) copy-start(s32[8,7]{1,0:T(8,128)} %param.18) | copy-start | bytes 676
  126.6 71.6 %all-gather.10.cloned.1.call-start = ((), (), s32[]{:S(2)}) async-start(), calls=%async_computation.5 | async-start | bytes 4128768 | tf_op jit(solution)/shard_map/all_gather | solution.py:44
  127.2 125.2 %all-gather.12.cloned.1.call-start = ((), (), s32[]{:S(2)}) async-start(), calls=%async_computation.7 | async-start | bytes 4456448 | tf_op jit(solution)/shard_map/all_gather | solution.py:55
  127.8 160.1 %all-gather.14.cloned.1.call-start = ((), (), s32[]{:S(2)}) async-start(), calls=%async_computation.8 | async-start | bytes 4128768 | tf_op jit(solution)/shard_map/all_gather | solution.py:42
  128.4 247.1 %reduce-scatter.5.cloned.1.call-start = ((), (), s32[]{:S(2)}) async-start(), calls=%async_computation.6 | async-start | bytes 8912896 | tf_op jit(solution)/shard_map/reduce_scatter | solution.py:47
  135.7 2.2 copy-start
Sparse Core Ops, SparseCore 0:
  10.1 54.8 all-gather.5
  77.3 46.4 reduce-scatter.2
  126.7 34.4 all-gather.7
  163.3 34.8 all-gather.9
  200.2 52.1 all-gather.11
  253.9 33.8 all-gather.13
  291.2 84.1 reduce-scatter.4
where the time goes:
time: 385 us; the launch traced here: 384 us
  waiting for transfers between devices  292 us (76%)
  matrix products  54.2 us (14%)
  local copies, waits for them, and re-layouts  16.6 us (4%)
  between operations  14.2 us (4%)
  other arithmetic  6.74 us (2%)
    reduce_scatter x1, waiting for transfers between devices, per_device(): lax.psum_scatter(first + lax.dot_general(grad_u_all, up_eff, contract, pr...  78.6 us
    all_gather x1, waiting for transfers between devices, per_device(): grad_all = lax.all_gather(grad_out, 'col', axis=0, tiled=True)  56.4 us
    reduce_scatter x1, waiting for transfers between devices, per_device(): lax.psum_scatter(lax.dot_general(grad_all, down_eff, contract, preferred_...  45.2 us
    all_gather x1, waiting for transfers between devices, per_device(): input_all = lax.all_gather(inputs, 'col', axis=0, tiled=True)  44 us
    all_gather x1, waiting for transfers between devices, per_device(): lax.all_gather(grad_u, 'row', axis=0, tiled=True)  26.5 us
    all_gather x1, waiting for transfers between devices, per_device(): lax.all_gather(grad_g, 'row', axis=0, tiled=True)  23.2 us
    all_gather x1, waiting for transfers between devices, per_device(): lax.all_gather(act, 'row', axis=0, tiled=True)  15.6 us
    unnamed x22, local copies, waits for them, and re-layouts  15.3 us
  transfers between devices with their start and end apart: 7, of which 7 were waited for; matrix products, arithmetic and copies ran while one was open for 15% of the time, Pallas kernels for 0%

commit v1 on v0

v1 whole, which is shorter than its diff:
```python
import jax
import jax.numpy as jnp
from jax import lax
from jax.experimental import pallas as pl
from jax.experimental.pallas import tpu as pltpu
from jax.sharding import PartitionSpec as P

MESH = pl.DeviceIdType.MESH
BF = jnp.bfloat16
F32 = jnp.float32
NT = (((1,), (1,)), ((), ()))
TN = (((0,), (0,)), ((), ()))
RELS = (2, 1, -1, 0)
GROUPS = (0, 1, -1, 2)


def m4(value):
    return lax.rem(value + 8, 4)


def coords():
    row, col = lax.axis_index("row"), lax.axis_index("col")
    return lax.div(row, 2), lax.rem(row, 2), lax.div(col, 4), lax.rem(col, 4)


def device(y, k, x, z):
    return {"row": y * 2 + k, "col": x * 4 + z}


def remote(src, dst, send, recv, to):
    return pltpu.make_async_remote_copy(
        src_ref=src, dst_ref=dst, send_sem=send, recv_sem=recv, device_id=to, device_id_type=MESH
    )


class ColGather:
    def __init__(self, full, send, recv):
        self.full, self.send_sem, self.recv_sem = full, send, recv
        self.y, self.k, self.x, self.z = coords()

    def piece(self, q, c):
        return self.full.at[c, pl.ds(pl.multiple_of(q * 32, 32), 32)]

    def index(self, q, a, b):
        late = lax.div(q, 2)
        return m4(self.x + a * (1 - late) + b * late) * 4 + m4(self.z + a * late + b * (1 - late))

    def send(self, q, a, b, second, d, slot):
        c = self.index(q, a, b)
        late = lax.div(q, 2)
        along_z = late + second - 2 * late * second
        to = device(self.y, self.k, m4(self.x + d * (1 - along_z)), m4(self.z + d * along_z))
        remote(
            self.piece(q, c), self.piece(q, c), self.send_sem.at[q * 15 + slot], self.recv_sem.at[q, c], to
        ).start()

    def recv(self, q, a, b):
        c = self.index(q, a, b)
        remote(
            self.piece(q, c),
            self.piece(q, c),
            self.send_sem.at[0],
            self.recv_sem.at[q, c],
            device(self.y, self.k, m4(self.x + 1), self.z),
        ).wait_recv()

    def each(self, body):
        def step(q, carry):
            body(q, 1 - 2 * lax.rem(q, 2))
            return carry

        lax.fori_loop(0, 4, step, 0)

    def start(self):
        def own(q, w):
            self.send(q, 0, 0, 0, 1, 0)
            self.send(q, 0, 0, 0, -1, 1)

        def own_second(q, w):
            self.send(q, 0, 0, 1, 1, 2)
            self.send(q, 0, 0, 1, -1, 3)

        self.each(own)
        self.each(own_second)

    def steps(self):
        def first(q, w):
            self.recv(q, -w, 0)
            self.send(q, -w, 0, 0, w, 4)
            self.send(q, -w, 0, 1, 1, 5)
            self.send(q, -w, 0, 1, -1, 6)

        def second(q, w):
            self.recv(q, w, 0)
            self.send(q, w, 0, 1, 1, 7)
            self.send(q, w, 0, 1, -1, 8)

        def own_line(q, w):
            self.recv(q, 0, -w)
            self.send(q, 0, -w, 1, w, 9)

        def far(q, w):
            self.recv(q, 2, 0)
            self.send(q, 2, 0, 1, 1, 10)
            self.send(q, 2, 0, 1, -1, 11)

        for body in (first, second, own_line, far):
            self.each(body)
            yield
        for slot, a in ((12, -1), (13, 1), (14, 2)):

            def line(q, w, a=a, slot=slot):
                self.recv(q, a * w, -w)
                self.send(q, a * w, -w, 1, w, slot)

            self.each(line)
            yield
        for a in (0, -1, 1, 2):

            def last(q, w, a=a):
                self.recv(q, a * w, w)
                self.recv(q, a * w, 2)

            self.each(last)
            yield

    def finish(self):
        def one(i, carry):
            remote(
                self.piece(0, 0),
                self.piece(0, 0),
                self.send_sem.at[i],
                self.recv_sem.at[0, 0],
                device(self.y, self.k, m4(self.x + 1), self.z),
            ).wait_send()
            return carry

        lax.fori_loop(0, 60, one, 0)


class RowGather:
    def __init__(self, view, send, recv):
        self.view, self.send_sem, self.recv_sem = view, send, recv
        self.y, self.k, self.x, self.z = coords()

    def row(self, dy, sibling=False):
        return m4(self.y + dy) * 2 + (1 - self.k if sibling else self.k)

    def sibling(self):
        return device(self.y, 1 - self.k, self.x, self.z)

    def copy(self, h, r, slot, to):
        return remote(self.view(r, h), self.view(r, h), self.send_sem.at[h * 7 + slot], self.recv_sem.at[h, r], to)

    def ring(self, h, dy, d, slot):
        to = device(m4(self.y + d), self.k, self.x, self.z)
        self.copy(h, self.row(dy), slot, to).start()

    def cross(self, h, dy, slot):
        self.copy(h, self.row(dy), slot, self.sibling()).start()

    def recv(self, h, dy, sibling=False):
        self.copy(h, self.row(dy, sibling), 0, self.sibling()).wait_recv()

    def start_half(self, h):
        self.ring(h, 0, 1, 0)
        self.ring(h, 0, -1, 1)
        self.cross(h, 0, 2)

    def start(self):
        for h in (0, 1):
            self.start_half(h)

    def near(self):
        for h in (0, 1):
            w = 1 - 2 * h
            self.recv(h, -w)
            self.ring(h, -w, w, 3)
            self.cross(h, -w, 4)

    def other(self):
        for h in (0, 1):
            w = 1 - 2 * h
            self.recv(h, w)
            self.cross(h, w, 5)

    def far(self):
        for h in (0, 1):
            self.recv(h, 2)
            self.cross(h, 2, 6)

    def from_sibling(self, dy):
        for h in (0, 1):
            self.recv(h, dy, True)

    def finish(self):
        for h in (0, 1):
            for slot in range(7):
                self.copy(h, 0, slot, self.sibling()).wait_send()


def kernel(
    x_in, dy_in, g_in, u_in, wg_in, wu_in, wd_in, mg, mu, md,
    gi_out, gg_out, gu_out, gd_out,
    dy, xx, ga, ua, hd, act, wg, wu, wd, hp, rb, ys, yr, s1, r1, s2, r2, gi, stage,
    lsem, osem, col_s, col_r, row_s, row_r, sib_s, sib_r, ring_s, ring_r, gs, gr,
):
    y, k, x, z = coords()
    me_col, me_row = x * 4 + z, y * 2 + k
    sibling = device(y, 1 - k, x, z)
    up_y, down_y = device(m4(y + 1), k, x, z), device(m4(y - 1), k, x, z)

    local = [
        pltpu.make_async_copy(dy_in, dy.at[me_col], lsem.at[0]),
        pltpu.make_async_copy(g_in.at[pl.ds(0, 128)], ga.at[2 * me_row], lsem.at[1]),
        pltpu.make_async_copy(g_in.at[pl.ds(128, 128)], ga.at[2 * me_row + 1], lsem.at[2]),
        pltpu.make_async_copy(u_in.at[pl.ds(0, 128)], ua.at[2 * me_row], lsem.at[3]),
        pltpu.make_async_copy(u_in.at[pl.ds(128, 128)], ua.at[2 * me_row + 1], lsem.at[4]),
        pltpu.make_async_copy(wd_in, wd, lsem.at[5]),
        pltpu.make_async_copy(x_in, xx.at[me_col], lsem.at[6]),
        pltpu.make_async_copy(wg_in, wg, lsem.at[7]),
        pltpu.make_async_copy(wu_in, wu, lsem.at[8]),
    ]
    for copy in local:
        copy.start()

    barrier = pltpu.get_barrier_semaphore()
    for to in (
        device(y, k, m4(x + 1), z),
        device(y, k, m4(x - 1), z),
        device(y, k, x, m4(z + 1)),
        device(y, k, x, m4(z - 1)),
        up_y,
        down_y,
        sibling,
    ):
        pl.semaphore_signal(barrier, inc=1, device_id=to, device_id_type=MESH)
    pl.semaphore_wait(barrier, 7)

    dy_gather = ColGather(dy, col_s.at[0], col_r.at[0])
    x_gather = ColGather(xx, col_s.at[1], col_r.at[1])
    g_gather = RowGather(lambda r, h: ga.at[2 * r + h], row_s.at[0], row_r.at[0])
    u_gather = RowGather(lambda r, h: ua.at[2 * r + h], row_s.at[1], row_r.at[1])
    h_gather = RowGather(lambda r, h: hd.at[r, h], row_s.at[2], row_r.at[2])
    dy_steps, x_steps = dy_gather.steps(), x_gather.steps()

    def advance(steps, count):
        for _ in range(count):
            next(steps, None)

    def apply_mask(w, mask, rows, columns):
        def line(i, carry):
            here = pl.ds(pl.multiple_of(i * 128, 128), 128)
            for j in range(columns):
                keep = mask[i, j].astype(F32)
                block = w[here, j * 128 : (j + 1) * 128].astype(F32)
                w[here, j * 128 : (j + 1) * 128] = (block * keep).astype(BF)
            return carry

        lax.fori_loop(0, rows, line, 0)

    local[0].wait()
    dy_gather.start()
    for copy in local[1:5]:
        copy.wait()
    g_gather.start()
    u_gather.start()
    local[5].wait()
    apply_mask(wd, md, 7, 8)

    advance(dy_steps, 7)
    g_gather.near()
    local[6].wait()
    x_gather.start()
    advance(dy_steps, 4)
    u_gather.near()

    def across(slot):
        there = pl.ds(2 * (1 - k), 2)
        return remote(
            hp.at[slot, there, :, :, pl.ds(0, 896)], rb.at[slot], sib_s.at[slot], sib_r.at[slot], sibling
        )

    def partial(slot):
        j = m4(y + RELS[slot])
        rows = pl.ds(pl.multiple_of(j * 32, 32), 32)
        left = dy[:, rows, :].reshape(512, 1024)
        product = lax.dot_general(left, wd[...], NT, preferred_element_type=F32)
        hp[slot, :, :, :, 0:896] = product.reshape(4, 4, 32, 896)
        across(slot).start()

    def total(slot, h, i):
        return hp[slot, 2 * k + h, i, :, 0:896] + rb[slot, h, i]

    def ring_copy(n, to):
        return remote(ys.at[n], yr.at[n], ring_s.at[n], ring_r.at[n], to)

    def pack(n, slot, h, with_recv=None):
        def one(i, carry):
            value = total(slot, h, i)
            if with_recv is not None:
                value = value + yr[with_recv, i].astype(F32)
            ys[n, i] = value.astype(BF)
            return carry

        lax.fori_loop(0, 4, one, 0)

    partial(0)
    partial(1)
    across(0).wait_recv()
    pack(0, 0, 0)
    ring_copy(0, up_y).start()
    pack(1, 0, 1)
    ring_copy(1, down_y).start()
    partial(2)
    advance(x_steps, 1)
    across(1).wait_recv()
    pack(2, 1, 1)
    ring_copy(2, up_y).start()
    partial(3)
    across(2).wait_recv()
    pack(3, 2, 0)
    ring_copy(3, down_y).start()
    advance(x_steps, 1)

    local[7].wait()
    apply_mask(wg, mg, 8, 7)
    advance(x_steps, 1)
    g_gather.other()
    u_gather.other()
    local[8].wait()
    apply_mask(wu, mu, 8, 7)
    advance(x_steps, 1)
    g_gather.far()
    u_gather.far()
    advance(x_steps, 1)

    for offset in (0, 1, -1, 2):
        g_gather.from_sibling(offset)
        u_gather.from_sibling(offset)

    def activation(lo, hi):
        def one(c, carry):
            for part in range(4):
                rows = pl.ds(part * 32, 32)
                gated = ga[c, rows].astype(F32)
                act[c, rows] = (gated * jax.nn.sigmoid(gated) * ua[c, rows].astype(F32)).astype(BF)
            return carry

        lax.fori_loop(lo, hi, one, 0)

    activation(0, 8)
    advance(x_steps, 1)
    activation(8, 16)
    advance(x_steps, 1)

    ring_copy(0, up_y).wait_recv()
    pack(4, 1, 0, 0)
    ring_copy(4, up_y).start()
    ring_copy(1, up_y).wait_recv()
    pack(5, 2, 1, 1)
    ring_copy(5, down_y).start()

    outs = []

    def emit(slot, rows, columns, out, at):
        if len(outs) >= 4:
            outs[len(outs) - 4].wait()
        copy = pltpu.make_async_copy(
            stage.at[slot, pl.ds(0, rows), pl.ds(0, columns)], out.at[pl.ds(at, rows)], osem.at[slot]
        )
        return copy

    def weight_tile(left, right, mask, out, i, rows, columns):
        slot = len(outs) % 4
        copy = emit(slot, rows, columns, out, i * 256)
        a = left[:, :, i * 256 : i * 256 + rows].reshape(2048, rows)
        b = right[...].reshape(2048, columns)
        product = lax.dot_general(a, b, TN, preferred_element_type=F32)
        for p in range(rows // 128):
            for q in range(columns // 128):
                keep = mask[i * 2 + p, q].astype(F32)
                block = product[p * 128 : (p + 1) * 128, q * 128 : (q + 1) * 128]
                stage[slot, p * 128 : (p + 1) * 128, q * 128 : (q + 1) * 128] = (block * keep).astype(BF)
        copy.start()
        outs.append(copy)

    weight_tile(act, dy, md, gd_out, 0, 256, 1024)
    advance(x_steps, 1)
    weight_tile(act, dy, md, gd_out, 1, 256, 1024)
    advance(x_steps, 1)

    across(3).wait_recv()
    ring_copy(3, up_y).wait_recv()
    ring_copy(2, up_y).wait_recv()

    def finish_hidden(h, first, second):
        def one(i, carry):
            value = total(3, h, i) + yr[first, i].astype(F32) + yr[second, i].astype(F32)
            hd[me_row, h, i] = value.astype(BF)
            return carry

        lax.fori_loop(0, 4, one, 0)
        h_gather.start_half(h)

    ring_copy(4, up_y).wait_recv()
    finish_hidden(0, 4, 3)
    ring_copy(5, up_y).wait_recv()
    finish_hidden(1, 2, 5)
    for n in range(6):
        ring_copy(n, up_y).wait_send()
    for slot in range(4):
        across(slot).wait_send()
    g_gather.finish()
    u_gather.finish()

    def along(t, stage_at, d):
        if (t < 2) == (stage_at == 0):
            return device(y, k, x, m4(z + d))
        return device(y, k, m4(x + d), z)

    def group_copy(n, t, stage_at, kind):
        w = 1 - 2 * (t % 2)
        to = along(t, stage_at, -w if kind == 1 else w)
        at = n * 4 + t
        src, dst = (s1, r1) if stage_at == 0 else (s2, r2)
        return remote(
            src.at[at, kind], dst.at[at, kind], gs.at[at, stage_at, kind], gr.at[at, stage_at, kind], to
        )

    def columns(t):
        return pl.ds(t * 256, 256)

    def slab(n, t, d):
        if t < 2:
            return hp[n, :, m4(z + d), :, columns(t)]
        return hp[n, m4(x + d), :, :, columns(t)]

    def group_partial(n):
        j = m4(y + GROUPS[n])
        rows = pl.ds(pl.multiple_of(j * 32, 32), 32)

        def one(c, carry):
            gated = ga[c, rows].astype(F32)
            upper = ua[c, rows].astype(F32)
            hidden = hd[2 * j + lax.div(c, 8), lax.rem(lax.div(c, 4), 2), lax.rem(c, 4)].astype(F32)
            sigma = jax.nn.sigmoid(gated)
            ga[c, rows] = (hidden * upper * sigma * (1.0 + gated * (1.0 - sigma))).astype(BF)
            ua[c, rows] = (hidden * gated * sigma).astype(BF)
            return carry

        lax.fori_loop(0, 16, one, 0)
        product = lax.dot_general(ga[:, rows, :].reshape(512, 896), wg[...], NT, preferred_element_type=F32)
        product = product + lax.dot_general(
            ua[:, rows, :].reshape(512, 896), wu[...], NT, preferred_element_type=F32
        )
        hp[n] = product.reshape(4, 4, 32, 1024)
        for t in range(4):
            w = 1 - 2 * (t % 2)
            s1[n * 4 + t, 0] = slab(n, t, 2).astype(BF)
            group_copy(n, t, 0, 0).start()
        for t in range(4):
            w = 1 - 2 * (t % 2)
            s1[n * 4 + t, 1] = slab(n, t, -w).astype(BF)
            group_copy(n, t, 0, 1).start()

    def group_combine(n):
        for t in range(4):
            w = 1 - 2 * (t % 2)
            at = n * 4 + t
            group_copy(n, t, 0, 0).wait_recv()
            s1[at, 2] = (slab(n, t, w) + r1[at, 0].astype(F32)).astype(BF)
            group_copy(n, t, 0, 2).start()

    def line_total(n, t, d):
        at = n * 4 + t
        if t < 2:
            to = m4(x + d)
            own = hp[n, to, z, :, columns(t)]
        else:
            to = m4(z + d)
            own = hp[n, x, to, :, columns(t)]
        return own + r1[at, 1, to].astype(F32) + r1[at, 2, to].astype(F32)

    def group_second(n):
        for t in range(4):
            w = 1 - 2 * (t % 2)
            at = n * 4 + t
            group_copy(n, t, 0, 1).wait_recv()
            group_copy(n, t, 0, 2).wait_recv()
            s2[at, 0] = line_total(n, t, 2).astype(BF)
            group_copy(n, t, 1, 0).start()
            s2[at, 1] = line_total(n, t, -w).astype(BF)
            group_copy(n, t, 1, 1).start()

    def group_second_combine(n):
        for t in range(4):
            w = 1 - 2 * (t % 2)
            at = n * 4 + t
            group_copy(n, t, 1, 0).wait_recv()
            s2[at, 2] = (line_total(n, t, w) + r2[at, 0].astype(F32)).astype(BF)
            group_copy(n, t, 1, 2).start()

    def group_last(n):
        j = m4(y + GROUPS[n])
        rows = pl.ds(pl.multiple_of(j * 32, 32), 32)
        for t in range(4):
            at = n * 4 + t
            group_copy(n, t, 1, 1).wait_recv()
            group_copy(n, t, 1, 2).wait_recv()
            value = line_total(n, t, 0) + r2[at, 1].astype(F32) + r2[at, 2].astype(F32)
            gi[rows, columns(t)] = value.astype(BF)

    h_gather.from_sibling(0)
    group_partial(0)
    advance(x_steps, 2)
    h_gather.near()
    h_gather.other()
    group_combine(0)
    h_gather.from_sibling(1)
    group_partial(1)
    group_second(0)
    h_gather.from_sibling(-1)
    group_partial(2)
    group_combine(1)
    group_second_combine(0)
    h_gather.far()
    h_gather.from_sibling(2)
    group_partial(3)
    group_combine(2)
    group_second(1)
    group_combine(3)
    group_last(0)
    advance(x_steps, 4)
    weight_tile(xx, ga, mg, gg_out, 0, 256, 896)
    group_second(2)
    group_second_combine(1)
    group_second(3)
    weight_tile(xx, ga, mg, gg_out, 1, 256, 896)
    group_second_combine(2)
    group_second_combine(3)
    weight_tile(xx, ga, mg, gg_out, 2, 256, 896)
    group_last(1)
    weight_tile(xx, ga, mg, gg_out, 3, 256, 896)
    group_last(2)
    group_last(3)
    gi_copy = pltpu.make_async_copy(gi, gi_out, lsem.at[0])
    gi_copy.start()
    for i in range(4):
        weight_tile(xx, ua, mu, gu_out, i, 256, 896)
    weight_tile(act, dy, md, gd_out, 2, 256, 1024)
    weight_tile(act, dy, md, gd_out, 3, 128, 1024)

    for copy in outs[-4:]:
        copy.wait()
    gi_copy.wait()
    dy_gather.finish()
    x_gather.finish()
    h_gather.finish()

    def drain(at, carry):
        for kind in range(3):
            remote(s1.at[0, 0], r1.at[0, 0], gs.at[at, 0, kind], gr.at[0, 0, 0], sibling).wait_send()
            remote(s2.at[0, 0], r2.at[0, 0], gs.at[at, 1, kind], gr.at[0, 1, 0], sibling).wait_send()
        return carry

    lax.fori_loop(0, 16, drain, 0)


def per_device(
    inputs, grad_out, gate_pre, up_pre, w_gate, w_up, w_down, mask_gate, mask_up, mask_down
):
    anywhere = pl.BlockSpec(memory_space=pl.ANY)
    scalars = pl.BlockSpec(memory_space=pltpu.SMEM)
    dma = pltpu.SemaphoreType.DMA
    flops = 2 * 2048 * 1024 * 896 * 6
    return pl.pallas_call(
        kernel,
        out_shape=[
            jax.ShapeDtypeStruct((128, 1024), BF),
            jax.ShapeDtypeStruct((1024, 896), BF),
            jax.ShapeDtypeStruct((1024, 896), BF),
            jax.ShapeDtypeStruct((896, 1024), BF),
        ],
        in_specs=[anywhere] * 7 + [scalars] * 3,
        out_specs=[anywhere] * 4,
        scratch_shapes=[
            pltpu.VMEM((16, 128, 1024), BF),
            pltpu.VMEM((16, 128, 1024), BF),
            pltpu.VMEM((16, 128, 896), BF),
            pltpu.VMEM((16, 128, 896), BF),
            pltpu.VMEM((8, 2, 4, 32, 896), BF),
            pltpu.VMEM((16, 128, 896), BF),
            pltpu.VMEM((1024, 896), BF),
            pltpu.VMEM((1024, 896), BF),
            pltpu.VMEM((896, 1024), BF),
            pltpu.VMEM((4, 4, 4, 32, 1024), F32),
            pltpu.VMEM((4, 2, 4, 32, 896), F32),
            pltpu.VMEM((6, 4, 32, 896), BF),
            pltpu.VMEM((6, 4, 32, 896), BF),
            pltpu.VMEM((16, 3, 4, 32, 256), BF),
            pltpu.VMEM((16, 3, 4, 32, 256), BF),
            pltpu.VMEM((16, 3, 32, 256), BF),
            pltpu.VMEM((16, 3, 32, 256), BF),
            pltpu.VMEM((128, 1024), BF),
            pltpu.VMEM((4, 256, 1024), BF),
            dma((9,)),
            dma((4,)),
            dma((2, 60)),
            dma((2, 4, 16)),
            dma((3, 14)),
            dma((3, 2, 8)),
            dma((4,)),
            dma((4,)),
            dma((6,)),
            dma((6,)),
            dma((16, 2, 3)),
            dma((16, 2, 3)),
        ],
        compiler_params=pltpu.CompilerParams(
            collective_id=0, has_side_effects=True, vmem_limit_bytes=62 * 2**20
        ),
        cost_estimate=pl.CostEstimate(flops=flops, bytes_accessed=18 * 2**20, transcendentals=4 * 2048 * 896),
    )(inputs, grad_out, gate_pre, up_pre, w_gate, w_up, w_down, mask_gate, mask_up, mask_down)


def solution(mesh):
    placed = (
        P("col", "row"),
        P("col", "row"),
        P("row", "col"),
        P("row", "col"),
        P("row", "col"),
        P("row", "col"),
        P("col", "row"),
        P("row", "col"),
        P("row", "col"),
        P("col", "row"),
    )
    return jax.shard_map(
        per_device,
        mesh=mesh,
        in_specs=placed,
        out_specs=(P("col", "row"), P("row", "col"), P("row", "col"), P("col", "row")),
        check_vma=False,
    )
```

time: 385 us -> 123 us (0.32)
  waiting for transfers between devices: 292 us -> 0 us
  Pallas kernels: 0 us -> 114 us
  matrix products: 54.2 us -> 0 us
  between operations: 14.2 us -> 0.65 us
  local copies, waits for them, and re-layouts: 16.6 us -> 8.07 us
  other arithmetic: 6.74 us -> 0 us
    all_gather x5 -> x0, waiting for transfers between devices: 166 us -> none  [the longest x1 56.4 us: per_device(): grad_all = lax.all_gather(grad_out, 'col', axis=0, tiled=True)]
    reduce_scatter x2 -> x0, waiting for transfers between devices: 124 us -> none  [the longest x1 78.6 us: per_device(): lax.psum_scatter(first + lax.dot_general(grad_u_all, up_eff, contract, pr...]
    pallas_call x0 -> x1, Pallas kernels: none -> 114 us  [per_device(): pl.pallas_call(kernel, out_shape=[jax.ShapeDtypeStruct((128, 1024), BF),...]
    dot_general x6 -> x0, matrix products: 54.2 us -> none  [the longest x1 10.4 us: per_device(): lax.dot_general(grad_g_all, gate_eff, contract, preferred_element_type=jn...]
    unnamed x22 -> x8, local copies, waits for them, and re-layouts: 15.3 us -> 8.07 us
    convert_element_type x5 -> x0, other arithmetic: 5.26 us -> none  [the longest x1 2.78 us: swiglu_grads(): grad_u = (hidden_grad * gated * sigma).astype(jnp.bfloat16)]
  transfers between devices with their start and end apart: 7 -> 0, of which waited for: 7 -> 0; matrix products, arithmetic and copies ran while one was open for 15% -> 0% of each run, Pallas kernels for 0% -> 0%
where the time goes in v1:
time: 123 us
  Pallas kernels  114 us (93%)
  local copies, waits for them, and re-layouts  8.07 us (7%)
    pallas_call x1, Pallas kernels, per_device(): pl.pallas_call(kernel, out_shape=[jax.ShapeDtypeStruct((128, 1024), BF),...  114 us
    unnamed x8, local copies, waits for them, and re-layouts  8.07 us

profile of v1, /device:TPU:1, one launch (start us, length us, event | category | flops | bytes accessed | tf_op | source)
XLA Modules:
  0.0 122.7 jit_solution(5332535900166317769)
XLA Ops:
  0.6 113.9 %shard_map.129 = (bf16[128,1024]{1,0:T(8,128)(2,1)}, bf16[1024,896]{1,0:T(8,128)(2,1)}, bf16[1024,896]{1,0:T(8,128)(2,1)}, bf16[896,1024]{1,0:T(8,128)(2,1)}) custom-call(bf16[128,1024]{1,0:T(8,128)(2,1)} %x_in.1, bf16[128,1024]{1,0:T(8,128)(2,1)} %dy_in.1, bf16[256,896]{1,0:T(8,128)(2,1)} %g_in.1, bf16[256,896]{1,0:T(8,128)(2,1)} %u_in.1, ...), custom_call_target="tpu_custom_call" | custom-call | flops 22548578304 | bytes 18874368 | tf_op jit(solution)/shard_map/pallas_call | solution.py:577
  114.6 1.7 %copy.18 = bf16[128,1024]{1,0:T(8,128)(2,1)} copy(bf16[128,1024]{1,0:T(8,128)(2,1)} %get-tuple-element.8) | data formatting | bytes 524288
  116.3 0.0 copy-start.1
  116.3 3.0 %copy.19 = bf16[1024,896]{1,0:T(8,128)(2,1)} copy(bf16[1024,896]{1,0:T(8,128)(2,1)} %get-tuple-element.9) | data formatting | bytes 3670016
  119.3 0.0 copy-done.1
  119.3 0.0 copy-start
  119.3 1.2 %copy.20 = bf16[1024,896]{1,0:T(8,128)(2,1)} copy(bf16[1024,896]{1,0:T(8,128)(2,1)S(1)} %copy-done.1) | data formatting | bytes 3670016
  120.5 0.9 copy-done
  121.4 1.2 %copy.21 = bf16[896,1024]{1,0:T(8,128)(2,1)} copy(bf16[896,1024]{1,0:T(8,128)(2,1)S(1)} %copy-done) | data formatting | bytes 3670016
Async XLA Ops:
  116.3 3.0 %copy-start.1 = (bf16[1024,896]{1,0:T(8,128)(2,1)S(1)}, bf16[1024,896]{1,0:T(8,128)(2,1)}, u32[]{:S(2)}) copy-start(bf16[1024,896]{1,0:T(8,128)(2,1)} %get-tuple-element.10) | copy-start | bytes 5505028
  119.3 2.2 %copy-start = (bf16[896,1024]{1,0:T(8,128)(2,1)S(1)}, bf16[896,1024]{1,0:T(8,128)(2,1)}, u32[]{:S(2)}) copy-start(bf16[896,1024]{1,0:T(8,128)(2,1)} %get-tuple-element.11) | copy-start | bytes 5505028

commit v2 on v0

v2 whole, which is shorter than its diff:
```python
import jax
import jax.numpy as jnp
from jax import lax
from jax.experimental import pallas as pl
from jax.experimental.pallas import tpu as pltpu
from jax.sharding import PartitionSpec as P

MESH = pl.DeviceIdType.MESH
BF = jnp.bfloat16
F32 = jnp.float32
NT = (((1,), (1,)), ((), ()))
TN = (((0,), (0,)), ((), ()))
RELS = (2, 1, -1, 0)
GROUPS = (0, 1, -1, 2)


def m4(value):
    return lax.rem(value + 8, 4)


def coords():
    row, col = lax.axis_index("row"), lax.axis_index("col")
    return lax.div(row, 2), lax.rem(row, 2), lax.div(col, 4), lax.rem(col, 4)


def device(y, k, x, z):
    return {"row": y * 2 + k, "col": x * 4 + z}


def remote(src, dst, send, recv, to):
    return pltpu.make_async_remote_copy(
        src_ref=src, dst_ref=dst, send_sem=send, recv_sem=recv, device_id=to, device_id_type=MESH
    )


class ColGather:
    def __init__(self, full, send, recv, at, rows):
        self.full, self.send_sem, self.recv_sem = full, send, recv
        self.at, self.rows = at, rows
        self.y, self.k, self.x, self.z = coords()

    def piece(self, q, c):
        return self.full.at[c, pl.ds(pl.multiple_of(q * 32 + self.at, 16), self.rows)]

    def index(self, q, a, b):
        late = lax.div(q, 2)
        return m4(self.x + a * (1 - late) + b * late) * 4 + m4(self.z + a * late + b * (1 - late))

    def send(self, q, a, b, second, d, slot):
        c = self.index(q, a, b)
        late = lax.div(q, 2)
        along_z = late + second - 2 * late * second
        to = device(self.y, self.k, m4(self.x + d * (1 - along_z)), m4(self.z + d * along_z))
        remote(
            self.piece(q, c), self.piece(q, c), self.send_sem.at[q * 15 + slot], self.recv_sem.at[q, c], to
        ).start()

    def recv(self, q, a, b):
        c = self.index(q, a, b)
        remote(
            self.piece(q, c),
            self.piece(q, c),
            self.send_sem.at[0],
            self.recv_sem.at[q, c],
            device(self.y, self.k, m4(self.x + 1), self.z),
        ).wait_recv()

    def each(self, body):
        def step(q, carry):
            body(q, 1 - 2 * lax.rem(q, 2))
            return carry

        lax.fori_loop(0, 4, step, 0)

    def start(self):
        def own(q, w):
            self.send(q, 0, 0, 0, 1, 0)
            self.send(q, 0, 0, 0, -1, 1)

        def own_second(q, w):
            self.send(q, 0, 0, 1, 1, 2)
            self.send(q, 0, 0, 1, -1, 3)

        self.each(own)
        self.each(own_second)

    def step(self, number):
        def first(q, w):
            self.recv(q, -w, 0)
            self.send(q, -w, 0, 0, w, 4)
            self.send(q, -w, 0, 1, 1, 5)
            self.send(q, -w, 0, 1, -1, 6)

        def second(q, w):
            self.recv(q, w, 0)
            self.send(q, w, 0, 1, 1, 7)
            self.send(q, w, 0, 1, -1, 8)

        def own_line(q, w):
            self.recv(q, 0, -w)
            self.send(q, 0, -w, 1, w, 9)

        def far(q, w):
            self.recv(q, 2, 0)
            self.send(q, 2, 0, 1, 1, 10)
            self.send(q, 2, 0, 1, -1, 11)

        def line(q, w):
            a = (-1, 1, 2)[number - 4]
            self.recv(q, a * w, -w)
            self.send(q, a * w, -w, 1, w, 8 + number)

        def last(q, w):
            a = (0, -1, 1, 2)[number - 7]
            self.recv(q, a * w, w)
            self.recv(q, a * w, 2)

        self.each((first, second, own_line, far, line, line, line, last, last, last, last)[number])

    def finish(self):
        def one(i, carry):
            remote(
                self.piece(0, 0),
                self.piece(0, 0),
                self.send_sem.at[i],
                self.recv_sem.at[0, 0],
                device(self.y, self.k, m4(self.x + 1), self.z),
            ).wait_send()
            return carry

        lax.fori_loop(0, 60, one, 0)


class RowGather:
    def __init__(self, view, send, recv):
        self.view, self.send_sem, self.recv_sem = view, send, recv
        self.y, self.k, self.x, self.z = coords()

    def row(self, dy, sibling=False):
        return m4(self.y + dy) * 2 + (1 - self.k if sibling else self.k)

    def sibling(self):
        return device(self.y, 1 - self.k, self.x, self.z)

    def copy(self, p, h, r, slot, to):
        view = self.view(r, p, h)
        return remote(view, view, self.send_sem.at[p * 14 + h * 7 + slot], self.recv_sem.at[p, h, r], to)

    def ring(self, p, h, dy, d, slot):
        to = device(m4(self.y + d), self.k, self.x, self.z)
        self.copy(p, h, self.row(dy), slot, to).start()

    def cross(self, p, h, dy, slot):
        self.copy(p, h, self.row(dy), slot, self.sibling()).start()

    def recv(self, p, h, dy, sibling=False):
        self.copy(p, h, self.row(dy, sibling), 0, self.sibling()).wait_recv()

    def start(self, p):
        self.ring(p, 0, 0, 1, 0)
        self.ring(p, 1, 0, -1, 1)
        self.ring(p, 1, 0, 1, 0)
        self.ring(p, 0, 0, -1, 1)
        self.cross(p, 0, 0, 2)
        self.cross(p, 1, 0, 2)

    def near(self, p):
        for h in (0, 1):
            w = 1 - 2 * h
            self.recv(p, h, -w)
            self.ring(p, h, -w, w, 3)
            self.cross(p, h, -w, 4)

    def other(self, p):
        for h in (0, 1):
            w = 1 - 2 * h
            self.recv(p, h, w)
            self.cross(p, h, w, 5)

    def far(self, p):
        for h in (0, 1):
            self.recv(p, h, 2)
            self.cross(p, h, 2, 6)

    def from_sibling(self, p, dy):
        for h in (0, 1):
            self.recv(p, h, dy, True)

    def finish(self, p):
        for h in (0, 1):
            for slot in range(7):
                self.copy(p, h, 0, slot, self.sibling()).wait_send()


def kernel(
    x_in, dy_in, g_in, u_in, wg_in, wu_in, wd_in, mg, mu, md,
    gi_out, gg_out, gu_out, gd_out,
    dy, xx, ga, ua, hd, act, wg, wu, wd, hp, pa, rb, ys, yr, s1, r1, s2, r2, gi, stage,
    lsem, osem, col_s, col_r, row_s, row_r, sib_s, sib_r, ring_s, ring_r, gs, gr,
):
    y, k, x, z = coords()
    me_col, me_row = x * 4 + z, y * 2 + k
    sibling = device(y, 1 - k, x, z)
    up_y, down_y = device(m4(y + 1), k, x, z), device(m4(y - 1), k, x, z)

    two = pl.ds(2 * me_row, 2)
    local = [
        pltpu.make_async_copy(dy_in, dy.at[me_col], lsem.at[0]),
        pltpu.make_async_copy(g_in, ga.at[two], lsem.at[1]),
        pltpu.make_async_copy(u_in, ua.at[two], lsem.at[2]),
        pltpu.make_async_copy(wd_in, wd, lsem.at[3]),
        pltpu.make_async_copy(x_in, xx.at[me_col], lsem.at[4]),
        pltpu.make_async_copy(wg_in, wg, lsem.at[5]),
        pltpu.make_async_copy(wu_in, wu, lsem.at[6]),
    ]
    for copy in local:
        copy.start()

    barrier = pltpu.get_barrier_semaphore()
    for to in (
        device(y, k, m4(x + 1), z),
        device(y, k, m4(x - 1), z),
        device(y, k, x, m4(z + 1)),
        device(y, k, x, m4(z - 1)),
        device(y, k, m4(x + 2), z),
        device(y, k, x, m4(z + 2)),
        up_y,
        down_y,
        sibling,
    ):
        pl.semaphore_signal(barrier, inc=1, device_id=to, device_id_type=MESH)
    pl.semaphore_wait(barrier, 9)

    dy_gathers = [ColGather(dy, col_s.at[p], col_r.at[p], 16 * p, 16) for p in range(2)]
    x_gather = ColGather(xx, col_s.at[2], col_r.at[2], 0, 32)
    g_gather = RowGather(lambda r, p, h: ga.at[2 * r + h, :, p], row_s.at[0], row_r.at[0])
    u_gather = RowGather(lambda r, p, h: ua.at[2 * r + h, :, p], row_s.at[1], row_r.at[1])
    h_gather = RowGather(lambda r, p, h: hd.at[r, p, h], row_s.at[2], row_r.at[2])

    def apply_mask(w, mask, rows, columns):
        def line(i, carry):
            here = pl.ds(pl.multiple_of(i * 128, 128), 128)
            for j in range(columns):
                keep = mask[i, j].astype(F32)
                block = w[here, j * 128 : (j + 1) * 128].astype(F32)
                w[here, j * 128 : (j + 1) * 128] = (block * keep).astype(BF)
            return carry

        lax.fori_loop(0, rows, line, 0)

    def across(p, slot):
        there, rows = pl.ds(2 * (1 - k), 2), pl.ds(16 * p, 16)
        return remote(
            hp.at[slot, there, :, rows, pl.ds(0, 896)],
            rb.at[slot, :, :, rows],
            sib_s.at[p, slot],
            sib_r.at[p, slot],
            sibling,
        )

    def partial(p, slot):
        j = m4(y + RELS[slot])
        rows = pl.ds(pl.multiple_of(j * 32 + p * 16, 16), 16)
        left = dy[:, rows, :].reshape(256, 1024)
        product = lax.dot_general(left, wd[...], NT, preferred_element_type=F32)
        hp[slot, :, :, p * 16 : p * 16 + 16, 0:896] = product.reshape(4, 4, 16, 896)
        across(p, slot).start()

    def total(p, slot, h, i):
        rows = pl.ds(p * 16, 16)
        return hp[slot, 2 * k + h, i, rows, 0:896] + rb[slot, h, i, rows]

    def ring_copy(p, n):
        to = up_y if n % 2 == 0 else down_y
        return remote(ys.at[p, n], yr.at[p, n], ring_s.at[p, n], ring_r.at[p, n], to)

    def pack(p, n, slot, h, with_recv=None):
        if with_recv is not None:
            ring_copy(p, with_recv).wait_recv()

        def one(i, carry):
            value = total(p, slot, h, i)
            if with_recv is not None:
                value = value + yr[p, with_recv, i].astype(F32)
            ys[p, n, i] = value.astype(BF)
            return carry

        lax.fori_loop(0, 4, one, 0)
        ring_copy(p, n).start()

    def pack_far(p):
        pack(p, 0, 0, 0)
        pack(p, 1, 0, 1)

    def pack_near(p):
        pack(p, 2, 1, 1)
        pack(p, 3, 2, 0)

    def pack_sum(p):
        pack(p, 4, 1, 0, 0)
        pack(p, 5, 2, 1, 1)

    def finish_hidden(p):
        for h, first, second in ((0, 3, 4), (1, 2, 5)):
            ring_copy(p, first).wait_recv()
            ring_copy(p, second).wait_recv()

            def one(i, carry, h=h, first=first, second=second):
                value = total(p, 3, h, i) + yr[p, first, i].astype(F32) + yr[p, second, i].astype(F32)
                hd[me_row, p, h, i] = value.astype(BF)
                return carry

            lax.fori_loop(0, 4, one, 0)
        h_gather.start(p)

    def activation(p):
        def one(c, carry):
            for j in range(4):
                gated = ga[c, j, p].astype(F32)
                act[c, j, p] = (gated * jax.nn.sigmoid(gated) * ua[c, j, p].astype(F32)).astype(BF)
            return carry

        lax.fori_loop(0, 16, one, 0)

    outs = []

    def weight_tile(left, right, mask, out, i, rows, columns):
        slot = len(outs) % 4
        if len(outs) >= 4:
            outs[len(outs) - 4].wait()
        copy = pltpu.make_async_copy(
            stage.at[slot, pl.ds(0, rows), pl.ds(0, columns)], out.at[pl.ds(i * 256, rows)], osem.at[slot]
        )
        if left is act:
            a = left[:, :, :, :, i * 256 : i * 256 + rows].reshape(2048, rows)
        else:
            a = left[:, :, i * 256 : i * 256 + rows].reshape(2048, rows)
        b = right[...].reshape(2048, columns)
        product = lax.dot_general(a, b, TN, preferred_element_type=F32)
        for p in range(rows // 128):
            for q in range(columns // 128):
                keep = mask[i * 2 + p, q].astype(F32)
                block = product[p * 128 : (p + 1) * 128, q * 128 : (q + 1) * 128]
                stage[slot, p * 128 : (p + 1) * 128, q * 128 : (q + 1) * 128] = (block * keep).astype(BF)
        copy.start()
        outs.append(copy)

    def down_tile(i):
        weight_tile(act, dy, md, gd_out, i, 256 if i < 3 else 128, 1024)

    def gate_tile(i):
        weight_tile(xx, ga, mg, gg_out, i, 256, 896)

    def up_tile(i):
        weight_tile(xx, ua, mu, gu_out, i, 256, 896)

    offsets = (2, 1, -1)

    def group_copy(p, n, t, stage_at, i):
        d = offsets[i]
        if t == stage_at:
            to = device(y, k, x, m4(z + d))
        else:
            to = device(y, k, m4(x + d), z)
        at = p * 8 + n * 2 + t
        src, dst = (s1, r1) if stage_at == 0 else (s2, r2)
        return remote(src.at[at, i], dst.at[at, i], gs.at[at, stage_at, i], gr.at[at, stage_at, i], to)

    def columns(t):
        return pl.ds(t * 512, 512)

    def partials(p):
        return pa if p == 0 else hp

    def group_partial(p, n):
        j = m4(y + GROUPS[n])

        def one(c, carry):
            gated = ga[c, j, p].astype(F32)
            upper = ua[c, j, p].astype(F32)
            hidden = hd[2 * j + lax.div(c, 8), p, lax.rem(lax.div(c, 4), 2), lax.rem(c, 4)].astype(F32)
            sigma = jax.nn.sigmoid(gated)
            ga[c, j, p] = (hidden * upper * sigma * (1.0 + gated * (1.0 - sigma))).astype(BF)
            ua[c, j, p] = (hidden * gated * sigma).astype(BF)
            return carry

        lax.fori_loop(0, 16, one, 0)
        product = lax.dot_general(ga[:, j, p].reshape(256, 896), wg[...], NT, preferred_element_type=F32)
        product = product + lax.dot_general(
            ua[:, j, p].reshape(256, 896), wu[...], NT, preferred_element_type=F32
        )
        partials(p)[n, :, :, 0:16, :] = product.reshape(4, 4, 16, 1024)
        for i, d in enumerate(offsets):
            s1[p * 8 + n * 2, i] = partials(p)[n, :, m4(z + d), 0:16, columns(0)].astype(BF)
            group_copy(p, n, 0, 0, i).start()
            s1[p * 8 + n * 2 + 1, i] = partials(p)[n, m4(x + d), :, 0:16, columns(1)].astype(BF)
            group_copy(p, n, 1, 0, i).start()

    def line_total(p, n, t, d):
        at = p * 8 + n * 2 + t
        if t == 0:
            to = m4(x + d)
            own = partials(p)[n, to, z, 0:16, columns(t)]
        else:
            to = m4(z + d)
            own = partials(p)[n, x, to, 0:16, columns(t)]
        for i in range(3):
            own = own + r1[at, i, to].astype(F32)
        return own

    def group_second(p, n):
        for t in range(2):
            for i in range(3):
                group_copy(p, n, t, 0, i).wait_recv()
        for i, d in enumerate(offsets):
            for t in range(2):
                s2[p * 8 + n * 2 + t, i] = line_total(p, n, t, d).astype(BF)
                group_copy(p, n, t, 1, i).start()

    def group_last(p, n):
        j = m4(y + GROUPS[n])
        rows = pl.ds(pl.multiple_of(j * 32 + p * 16, 16), 16)
        for t in range(2):
            value = line_total(p, n, t, 0)
            for i in range(3):
                group_copy(p, n, t, 1, i).wait_recv()
                value = value + r2[p * 8 + n * 2 + t, i].astype(F32)
            gi[rows, columns(t)] = value.astype(BF)

    local[0].wait()
    dy_gathers[0].start()
    local[1].wait()
    g_gather.start(0)
    local[2].wait()
    u_gather.start(0)
    local[3].wait()
    apply_mask(wd, md, 7, 8)
    local[5].wait()
    apply_mask(wg, mg, 8, 7)
    local[6].wait()
    apply_mask(wu, mu, 8, 7)
    dy_gathers[0].step(0)
    dy_gathers[1].start()
    dy_gathers[0].step(1)
    dy_gathers[0].step(2)
    g_gather.near(0)
    g_gather.other(0)
    dy_gathers[0].step(3)
    dy_gathers[0].step(4)
    dy_gathers[1].step(0)
    dy_gathers[1].step(1)
    u_gather.near(0)
    g_gather.start(1)
    u_gather.start(1)
    dy_gathers[1].step(2)
    dy_gathers[0].step(5)
    u_gather.other(0)
    dy_gathers[0].step(6)
    dy_gathers[0].step(7)
    g_gather.far(0)
    dy_gathers[0].step(8)
    dy_gathers[1].step(3)
    dy_gathers[1].step(4)
    dy_gathers[1].step(5)
    g_gather.near(1)
    dy_gathers[0].step(9)
    dy_gathers[0].step(10)
    partial(0, 0)
    partial(0, 1)
    dy_gathers[1].step(6)
    dy_gathers[1].step(7)
    local[4].wait()
    x_gather.start()
    dy_gathers[1].step(8)
    partial(0, 2)
    across(0, 0).wait_recv()
    pack_far(0)
    dy_gathers[1].step(9)
    partial(0, 3)
    u_gather.near(1)
    u_gather.far(0)
    g_gather.other(1)
    across(0, 1).wait_recv()
    across(0, 2).wait_recv()
    pack_near(0)
    dy_gathers[1].step(10)
    partial(1, 0)
    partial(1, 1)
    u_gather.other(1)
    for offset in (0, 1, -1, 2):
        g_gather.from_sibling(0, offset)
        u_gather.from_sibling(0, offset)
    activation(0)
    g_gather.finish(0)
    u_gather.finish(0)
    across(1, 0).wait_recv()
    pack_far(1)
    x_gather.step(0)
    x_gather.step(1)
    g_gather.far(1)
    partial(1, 2)
    partial(1, 3)
    x_gather.step(2)
    pack_sum(0)
    across(1, 1).wait_recv()
    across(1, 2).wait_recv()
    pack_near(1)
    u_gather.far(1)
    for offset in (0, 1, -1, 2):
        g_gather.from_sibling(1, offset)
        u_gather.from_sibling(1, offset)
    x_gather.step(3)
    x_gather.step(4)
    activation(1)
    g_gather.finish(1)
    u_gather.finish(1)
    down_tile(1)
    x_gather.step(5)
    down_tile(0)
    pack_sum(1)
    down_tile(3)
    across(0, 3).wait_recv()
    finish_hidden(0)
    down_tile(2)
    h_gather.from_sibling(0, 0)
    group_partial(0, 0)
    x_gather.step(6)
    x_gather.step(7)
    x_gather.step(8)
    x_gather.step(9)
    across(1, 3).wait_recv()
    finish_hidden(1)
    for p in range(2):
        for slot in range(4):
            across(p, slot).wait_send()
    h_gather.from_sibling(1, 0)
    group_partial(1, 0)
    h_gather.near(0)
    group_second(0, 0)
    h_gather.other(0)
    x_gather.step(10)
    h_gather.from_sibling(0, 1)
    group_partial(0, 1)
    h_gather.near(1)
    h_gather.from_sibling(0, -1)
    group_partial(0, 2)
    h_gather.other(1)
    group_second(1, 0)
    group_last(0, 0)
    h_gather.from_sibling(1, 1)
    group_partial(1, 1)
    h_gather.far(0)
    h_gather.from_sibling(1, -1)
    group_partial(1, 2)
    h_gather.far(1)
    h_gather.from_sibling(0, 2)
    group_partial(0, 3)
    h_gather.from_sibling(1, 2)
    group_partial(1, 3)
    group_second(1, 1)
    group_second(0, 2)
    group_second(0, 1)
    gate_tile(3)
    group_second(1, 2)
    group_last(1, 0)
    up_tile(3)
    up_tile(0)
    group_second(0, 3)
    up_tile(1)
    up_tile(2)
    group_second(1, 3)
    group_last(1, 1)
    gate_tile(0)
    group_last(0, 2)
    group_last(0, 1)
    group_last(1, 2)
    gate_tile(1)
    group_last(0, 3)
    gate_tile(2)
    group_last(1, 3)
    for p in range(2):
        for n in range(6):
            ring_copy(p, n).wait_send()

    gi_copy = pltpu.make_async_copy(gi, gi_out, lsem.at[0])
    gi_copy.start()
    for copy in outs[-4:]:
        copy.wait()
    gi_copy.wait()
    dy_gathers[0].finish()
    dy_gathers[1].finish()
    x_gather.finish()
    h_gather.finish(0)
    h_gather.finish(1)

    def drain(at, carry):
        for kind in range(3):
            remote(s1.at[0, 0], r1.at[0, 0], gs.at[at, 0, kind], gr.at[0, 0, 0], sibling).wait_send()
            remote(s2.at[0, 0], r2.at[0, 0], gs.at[at, 1, kind], gr.at[0, 1, 0], sibling).wait_send()
        return carry

    lax.fori_loop(0, 16, drain, 0)


def hand_over(*refs):
    sources, targets, held, come, gone = refs[:4], refs[4:8], refs[8:12], refs[12], refs[13]
    parts = []
    for source, target, hold in zip(sources, targets, held, strict=True):
        rows = source.shape[0] // 4
        for part in range(4):
            here, n = pl.ds(part * rows, rows), len(parts)
            parts.append(
                (
                    pltpu.make_async_copy(source.at[here], hold.at[here], come.at[n]),
                    pltpu.make_async_copy(hold.at[here], target.at[here], gone.at[n]),
                )
            )
    for first, _ in parts:
        first.start()
    for first, second in parts:
        first.wait()
        second.start()
    for _, second in parts:
        second.wait()


def per_device(
    inputs, grad_out, gate_pre, up_pre, w_gate, w_up, w_down, mask_gate, mask_up, mask_down
):
    anywhere = pl.BlockSpec(memory_space=pl.ANY)
    scalars = pl.BlockSpec(memory_space=pltpu.SMEM)
    dma = pltpu.SemaphoreType.DMA
    flops = 2 * 2048 * 1024 * 896 * 6
    shapes = [
        jax.ShapeDtypeStruct((128, 1024), BF),
        jax.ShapeDtypeStruct((1024, 896), BF),
        jax.ShapeDtypeStruct((1024, 896), BF),
        jax.ShapeDtypeStruct((896, 1024), BF),
    ]
    gate_parts = gate_pre.reshape(2, 4, 2, 16, 896)
    up_parts = up_pre.reshape(2, 4, 2, 16, 896)
    results = pl.pallas_call(
        kernel,
        out_shape=shapes,
        in_specs=[anywhere] * 7 + [scalars] * 3,
        out_specs=[anywhere] * 4,
        scratch_shapes=[
            pltpu.VMEM((16, 128, 1024), BF),
            pltpu.VMEM((16, 128, 1024), BF),
            pltpu.VMEM((16, 4, 2, 16, 896), BF),
            pltpu.VMEM((16, 4, 2, 16, 896), BF),
            pltpu.VMEM((8, 2, 2, 4, 16, 896), BF),
            pltpu.VMEM((16, 4, 2, 16, 896), BF),
            pltpu.VMEM((1024, 896), BF),
            pltpu.VMEM((1024, 896), BF),
            pltpu.VMEM((896, 1024), BF),
            pltpu.VMEM((4, 4, 4, 32, 1024), F32),
            pltpu.VMEM((4, 4, 4, 16, 1024), F32),
            pltpu.VMEM((4, 2, 4, 32, 896), F32),
            pltpu.VMEM((2, 6, 4, 16, 896), BF),
            pltpu.VMEM((2, 6, 4, 16, 896), BF),
            pltpu.VMEM((16, 3, 4, 16, 512), BF),
            pltpu.VMEM((16, 3, 4, 16, 512), BF),
            pltpu.VMEM((16, 3, 16, 512), BF),
            pltpu.VMEM((16, 3, 16, 512), BF),
            pltpu.VMEM((128, 1024), BF),
            pltpu.VMEM((4, 256, 1024), BF),
            dma((7,)),
            dma((4,)),
            dma((3, 60)),
            dma((3, 4, 16)),
            dma((3, 28)),
            dma((3, 2, 2, 8)),
            dma((2, 4)),
            dma((2, 4)),
            dma((2, 6)),
            dma((2, 6)),
            dma((16, 2, 3)),
            dma((16, 2, 3)),
        ],
        compiler_params=pltpu.CompilerParams(
            collective_id=0, has_side_effects=True, vmem_limit_bytes=62 * 2**20
        ),
        cost_estimate=pl.CostEstimate(flops=flops, bytes_accessed=18 * 2**20, transcendentals=4 * 2048 * 896),
    )(inputs, grad_out, gate_parts, up_parts, w_gate, w_up, w_down, mask_gate, mask_up, mask_down)
    return pl.pallas_call(
        hand_over,
        out_shape=shapes,
        in_specs=[anywhere] * 4,
        out_specs=[anywhere] * 4,
        scratch_shapes=[pltpu.VMEM(shape.shape, BF) for shape in shapes] + [dma((16,)), dma((16,))],
        compiler_params=pltpu.CompilerParams(vmem_limit_bytes=62 * 2**20),
        cost_estimate=pl.CostEstimate(flops=0, bytes_accessed=12 * 2**20, transcendentals=0),
    )(*results)


def solution(mesh):
    placed = (
        P("col", "row"),
        P("col", "row"),
        P("row", "col"),
        P("row", "col"),
        P("row", "col"),
        P("row", "col"),
        P("col", "row"),
        P("row", "col"),
        P("row", "col"),
        P("col", "row"),
    )
    return jax.shard_map(
        per_device,
        mesh=mesh,
        in_specs=placed,
        out_specs=(P("col", "row"), P("row", "col"), P("row", "col"), P("col", "row")),
        check_vma=False,
    )
```

time: 385 us -> 105 us (0.27)
  waiting for transfers between devices: 292 us -> 0 us
  Pallas kernels: 0 us -> 104 us
  matrix products: 54.2 us -> 0 us
  local copies, waits for them, and re-layouts: 16.6 us -> 0 us
  between operations: 14.2 us -> 0.8 us
  other arithmetic: 6.74 us -> 0 us
    all_gather x5 -> x0, waiting for transfers between devices: 166 us -> none  [the longest x1 56.4 us: per_device(): grad_all = lax.all_gather(grad_out, 'col', axis=0, tiled=True)]
    reduce_scatter x2 -> x0, waiting for transfers between devices: 124 us -> none  [the longest x1 78.6 us: per_device(): lax.psum_scatter(first + lax.dot_general(grad_u_all, up_eff, contract, pr...]
    pallas_call x0 -> x2, Pallas kernels: none -> 104 us  [the longest x1 98.4 us: per_device(): pl.pallas_call(kernel, out_shape=shapes, in_specs=[anywhere] * 7 + [scala...]
    dot_general x6 -> x0, matrix products: 54.2 us -> none  [the longest x1 10.4 us: per_device(): lax.dot_general(grad_g_all, gate_eff, contract, preferred_element_type=jn...]
    unnamed x22 -> x0, local copies, waits for them, and re-layouts: 15.3 us -> none
    convert_element_type x5 -> x0, other arithmetic: 5.26 us -> none  [the longest x1 2.78 us: swiglu_grads(): grad_u = (hidden_grad * gated * sigma).astype(jnp.bfloat16)]
  transfers between devices with their start and end apart: 7 -> 0, of which waited for: 7 -> 0; matrix products, arithmetic and copies ran while one was open for 15% -> 0% of each run, Pallas kernels for 0% -> 0%
where the time goes in v2:
time: 105 us
  Pallas kernels  104 us (99%)
    pallas_call x1, Pallas kernels, per_device(): pl.pallas_call(kernel, out_shape=shapes, in_specs=[anywhere] * 7 + [scala...  98.4 us
    pallas_call x1, Pallas kernels, per_device(): pl.pallas_call(hand_over, out_shape=shapes, in_specs=[anywhere] * 4, out_...  5.31 us

profile of v2, /device:TPU:1, one launch (start us, length us, event | category | flops | bytes accessed | tf_op | source)
XLA Modules:
  0.0 104.5 jit_solution(3236241203144358983)
XLA Ops:
  0.6 98.4 %shard_map.129 = (bf16[128,1024]{1,0:T(8,128)(2,1)}, bf16[1024,896]{1,0:T(8,128)(2,1)}, bf16[1024,896]{1,0:T(8,128)(2,1)}, bf16[896,1024]{1,0:T(8,128)(2,1)}) custom-call(bf16[128,1024]{1,0:T(8,128)(2,1)} %x_in.1, bf16[128,1024]{1,0:T(8,128)(2,1)} %dy_in.1, bf16[2,4,2,16,896]{4,3,2,1,0:T(8,128)(2,1)} %bitcast.2, bf16[2,4,2,16,896]{4,3,2,1,0:T(8,128)(2,1)} %bitcast.3, ...), custom_call_target="tpu_custom_call" | custom-call | flops 22548578304 | bytes 18874368 | tf_op jit(solution)/shard_map/pallas_call | solution.py:642
  99.0 5.3 %shard_map.130 = (bf16[128,1024]{1,0:T(8,128)(2,1)}, bf16[1024,896]{1,0:T(8,128)(2,1)}, bf16[1024,896]{1,0:T(8,128)(2,1)}, bf16[896,1024]{1,0:T(8,128)(2,1)}) custom-call(bf16[128,1024]{1,0:T(8,128)(2,1)} %get-tuple-element.8.refs_0_, bf16[1024,896]{1,0:T(8,128)(2,1)} %get-tuple-element.9.refs_1_, bf16[1024,896]{1,0:T(8,128)(2,1)} %get-tuple-element.10.refs_2_, ...), custom_call_target="tpu_custom_call" | custom-call | bytes 12582912 | tf_op jit(solution)/shard_map/pallas_call | solution.py:686

commit v3 on v2

--- a/solution.py
+++ b/solution.py
@@ -72,7 +72,7 @@
 
         lax.fori_loop(0, 4, step, 0)
 
-    def start(self):
+    def start(self, second):
         def own(q, w):
             self.send(q, 0, 0, 0, 1, 0)
             self.send(q, 0, 0, 0, -1, 1)
@@ -81,8 +81,7 @@
             self.send(q, 0, 0, 1, 1, 2)
             self.send(q, 0, 0, 1, -1, 3)
 
-        self.each(own)
-        self.each(own_second)
+        self.each(own_second if second else own)
 
     def step(self, number):
         def first(q, w):
@@ -156,13 +155,10 @@
     def recv(self, p, h, dy, sibling=False):
         self.copy(p, h, self.row(dy, sibling), 0, self.sibling()).wait_recv()
 
-    def start(self, p):
-        self.ring(p, 0, 0, 1, 0)
-        self.ring(p, 1, 0, -1, 1)
-        self.ring(p, 1, 0, 1, 0)
-        self.ring(p, 0, 0, -1, 1)
-        self.cross(p, 0, 0, 2)
-        self.cross(p, 1, 0, 2)
+    def start(self, p, second):
+        self.ring(p, second, 0, 1, 0)
+        self.ring(p, 1 - second, 0, -1, 1)
+        self.cross(p, second, 0, 2)
 
     def near(self, p):
         for h in (0, 1):
@@ -194,24 +190,24 @@
 
 def kernel(
     x_in, dy_in, g_in, u_in, wg_in, wu_in, wd_in, mg, mu, md,
-    gi_out, gg_out, gu_out, gd_out,
-    dy, xx, ga, ua, hd, act, wg, wu, wd, hp, pa, rb, ys, yr, s1, r1, s2, r2, gi, stage,
-    lsem, osem, col_s, col_r, row_s, row_r, sib_s, sib_r, ring_s, ring_r, gs, gr,
+    gi, gw, gd,
+    dy, xx, gu, hd, act, hp, pa, rb, ys, yr, s1, r1, s2, r2,
+    lsem, col_s, col_r, row_s, row_r, sib_s, sib_r, ring_s, ring_r, gs, gr,
 ):
     y, k, x, z = coords()
     me_col, me_row = x * 4 + z, y * 2 + k
     sibling = device(y, 1 - k, x, z)
     up_y, down_y = device(m4(y + 1), k, x, z), device(m4(y - 1), k, x, z)
 
-    two = pl.ds(2 * me_row, 2)
+    two, left_half, right_half = pl.ds(2 * me_row, 2), pl.ds(0, 896), pl.ds(896, 896)
     local = [
         pltpu.make_async_copy(dy_in, dy.at[me_col], lsem.at[0]),
-        pltpu.make_async_copy(g_in, ga.at[two], lsem.at[1]),
-        pltpu.make_async_copy(u_in, ua.at[two], lsem.at[2]),
-        pltpu.make_async_copy(wd_in, wd, lsem.at[3]),
+        pltpu.make_async_copy(g_in, gu.at[two, :, :, :, left_half], lsem.at[1]),
+        pltpu.make_async_copy(u_in, gu.at[two, :, :, :, right_half], lsem.at[2]),
+        pltpu.make_async_copy(wd_in, gd, lsem.at[3]),
         pltpu.make_async_copy(x_in, xx.at[me_col], lsem.at[4]),
-        pltpu.make_async_copy(wg_in, wg, lsem.at[5]),
-        pltpu.make_async_copy(wu_in, wu, lsem.at[6]),
+        pltpu.make_async_copy(wg_in, gw.at[:, left_half], lsem.at[5]),
+        pltpu.make_async_copy(wu_in, gw.at[:, right_half], lsem.at[6]),
     ]
     for copy in local:
         copy.start()
@@ -233,17 +229,16 @@
 
     dy_gathers = [ColGather(dy, col_s.at[p], col_r.at[p], 16 * p, 16) for p in range(2)]
     x_gather = ColGather(xx, col_s.at[2], col_r.at[2], 0, 32)
-    g_gather = RowGather(lambda r, p, h: ga.at[2 * r + h, :, p], row_s.at[0], row_r.at[0])
-    u_gather = RowGather(lambda r, p, h: ua.at[2 * r + h, :, p], row_s.at[1], row_r.at[1])
-    h_gather = RowGather(lambda r, p, h: hd.at[r, p, h], row_s.at[2], row_r.at[2])
-
-    def apply_mask(w, mask, rows, columns):
+    g_gather = RowGather(lambda r, p, h: gu.at[2 * r + h, :, p], row_s.at[0], row_r.at[0])
+    h_gather = RowGather(lambda r, p, h: hd.at[r, p, h], row_s.at[1], row_r.at[1])
+
+    def apply_mask(w, mask, rows, columns, first=0):
         def line(i, carry):
             here = pl.ds(pl.multiple_of(i * 128, 128), 128)
             for j in range(columns):
                 keep = mask[i, j].astype(F32)
-                block = w[here, j * 128 : (j + 1) * 128].astype(F32)
-                w[here, j * 128 : (j + 1) * 128] = (block * keep).astype(BF)
+                block = w[here, first + j * 128 : first + (j + 1) * 128].astype(F32)
+                w[here, first + j * 128 : first + (j + 1) * 128] = (block * keep).astype(BF)
             return carry
 
         lax.fori_loop(0, rows, line, 0)
@@ -262,7 +257,7 @@
         j = m4(y + RELS[slot])
         rows = pl.ds(pl.multiple_of(j * 32 + p * 16, 16), 16)
         left = dy[:, rows, :].reshape(256, 1024)
-        product = lax.dot_general(left, wd[...], NT, preferred_element_type=F32)
+        product = lax.dot_general(left, gd[...], NT, preferred_element_type=F32)
         hp[slot, :, :, p * 16 : p * 16 + 16, 0:896] = product.reshape(4, 4, 16, 896)
         across(p, slot).start()
 
@@ -311,48 +306,40 @@
                 return carry
 
             lax.fori_loop(0, 4, one, 0)
-        h_gather.start(p)
+        h_gather.start(p, 0)
+        h_gather.start(p, 1)
 
     def activation(p):
         def one(c, carry):
             for j in range(4):
-                gated = ga[c, j, p].astype(F32)
-                act[c, j, p] = (gated * jax.nn.sigmoid(gated) * ua[c, j, p].astype(F32)).astype(BF)
+                gated = gu[c, j, p, :, 0:896].astype(F32)
+                upper = gu[c, j, p, :, 896:1792].astype(F32)
+                act[c, j, p] = (gated * jax.nn.sigmoid(gated) * upper).astype(BF)
             return carry
 
         lax.fori_loop(0, 16, one, 0)
 
-    outs = []
-
-    def weight_tile(left, right, mask, out, i, rows, columns):
-        slot = len(outs) % 4
-        if len(outs) >= 4:
-            outs[len(outs) - 4].wait()
-        copy = pltpu.make_async_copy(
-            stage.at[slot, pl.ds(0, rows), pl.ds(0, columns)], out.at[pl.ds(i * 256, rows)], osem.at[slot]
-        )
-        if left is act:
-            a = left[:, :, :, :, i * 256 : i * 256 + rows].reshape(2048, rows)
-        else:
-            a = left[:, :, i * 256 : i * 256 + rows].reshape(2048, rows)
-        b = right[...].reshape(2048, columns)
-        product = lax.dot_general(a, b, TN, preferred_element_type=F32)
+    def keep_blocks(product, mask, out, i, rows, columns, first=0):
         for p in range(rows // 128):
             for q in range(columns // 128):
                 keep = mask[i * 2 + p, q].astype(F32)
-                block = product[p * 128 : (p + 1) * 128, q * 128 : (q + 1) * 128]
-                stage[slot, p * 128 : (p + 1) * 128, q * 128 : (q + 1) * 128] = (block * keep).astype(BF)
-        copy.start()
-        outs.append(copy)
+                at = first + q * 128
+                block = product[p * 128 : (p + 1) * 128, at : at + 128]
+                out[i * 256 + p * 128 : i * 256 + (p + 1) * 128, at : at + 128] = (block * keep).astype(BF)
 
     def down_tile(i):
-        weight_tile(act, dy, md, gd_out, i, 256 if i < 3 else 128, 1024)
-
-    def gate_tile(i):
-        weight_tile(xx, ga, mg, gg_out, i, 256, 896)
-
-    def up_tile(i):
-        weight_tile(xx, ua, mu, gu_out, i, 256, 896)
+        rows = 256 if i < 3 else 128
+        a = act[:, :, :, :, i * 256 : i * 256 + rows].reshape(2048, rows)
+        b = dy[...].reshape(2048, 1024)
+        product = lax.dot_general(a, b, TN, preferred_element_type=F32)
+        keep_blocks(product, md, gd, i, rows, 1024)
+
+    def pair_tile(i):
+        a = xx[:, :, i * 256 : (i + 1) * 256].reshape(2048, 256)
+        b = gu[...].reshape(2048, 1792)
+        product = lax.dot_general(a, b, TN, preferred_element_type=F32)
+        keep_blocks(product, mg, gw, i, 256, 896)
+        keep_blocks(product, mu, gw, i, 256, 896, 896)
 
     offsets = (2, 1, -1)
 
@@ -376,19 +363,16 @@
         j = m4(y + GROUPS[n])
 
         def one(c, carry):
-            gated = ga[c, j, p].astype(F32)
-            upper = ua[c, j, p].astype(F32)
+            gated = gu[c, j, p, :, 0:896].astype(F32)
+            upper = gu[c, j, p, :, 896:1792].astype(F32)
             hidden = hd[2 * j + lax.div(c, 8), p, lax.rem(lax.div(c, 4), 2), lax.rem(c, 4)].astype(F32)
             sigma = jax.nn.sigmoid(gated)
-            ga[c, j, p] = (hidden * upper * sigma * (1.0 + gated * (1.0 - sigma))).astype(BF)
-            ua[c, j, p] = (hidden * gated * sigma).astype(BF)
+            gu[c, j, p, :, 0:896] = (hidden * upper * sigma * (1.0 + gated * (1.0 - sigma))).astype(BF)
+            gu[c, j, p, :, 896:1792] = (hidden * gated * sigma).astype(BF)
             return carry
 
         lax.fori_loop(0, 16, one, 0)
-        product = lax.dot_general(ga[:, j, p].reshape(256, 896), wg[...], NT, preferred_element_type=F32)
-        product = product + lax.dot_general(
-            ua[:, j, p].reshape(256, 896), wu[...], NT, preferred_element_type=F32
-        )
+        product = lax.dot_general(gu[:, j, p].reshape(256, 1792), gw[...], NT, preferred_element_type=F32)
         partials(p)[n, :, :, 0:16, :] = product.reshape(4, 4, 16, 1024)
         for i, d in enumerate(offsets):
             s1[p * 8 + n * 2, i] = partials(p)[n, :, m4(z + d), 0:16, columns(0)].astype(BF)
@@ -428,106 +412,100 @@
             gi[rows, columns(t)] = value.astype(BF)
 
     local[0].wait()
-    dy_gathers[0].start()
+    dy_gathers[0].start(0)
+    dy_gathers[0].start(1)
     local[1].wait()
-    g_gather.start(0)
     local[2].wait()
-    u_gather.start(0)
-    local[3].wait()
-    apply_mask(wd, md, 7, 8)
-    local[5].wait()
-    apply_mask(wg, mg, 8, 7)
-    local[6].wait()
-    apply_mask(wu, mu, 8, 7)
+    g_gather.start(0, 0)
+    g_gather.start(0, 1)
+    g_gather.start(1, 0)
+    g_gather.start(1, 1)
     dy_gathers[0].step(0)
-    dy_gathers[1].start()
     dy_gathers[0].step(1)
+    dy_gathers[1].start(0)
+    dy_gathers[1].start(1)
+    local[4].wait()
+    x_gather.start(0)
     dy_gathers[0].step(2)
     g_gather.near(0)
-    g_gather.other(0)
     dy_gathers[0].step(3)
     dy_gathers[0].step(4)
+    dy_gathers[0].step(5)
+    local[3].wait()
+    apply_mask(gd, md, 7, 8)
+    local[5].wait()
+    apply_mask(gw, mg, 8, 7)
+    local[6].wait()
+    apply_mask(gw, mu, 8, 7, 896)
     dy_gathers[1].step(0)
     dy_gathers[1].step(1)
-    u_gather.near(0)
-    g_gather.start(1)
-    u_gather.start(1)
+    g_gather.other(0)
     dy_gathers[1].step(2)
-    dy_gathers[0].step(5)
-    u_gather.other(0)
+    g_gather.near(1)
     dy_gathers[0].step(6)
     dy_gathers[0].step(7)
-    g_gather.far(0)
     dy_gathers[0].step(8)
+    dy_gathers[0].step(9)
     dy_gathers[1].step(3)
+    x_gather.start(1)
     dy_gathers[1].step(4)
+    g_gather.other(1)
     dy_gathers[1].step(5)
-    g_gather.near(1)
-    dy_gathers[0].step(9)
     dy_gathers[0].step(10)
     partial(0, 0)
     partial(0, 1)
     dy_gathers[1].step(6)
     dy_gathers[1].step(7)
-    local[4].wait()
-    x_gather.start()
-    dy_gathers[1].step(8)
     partial(0, 2)
     across(0, 0).wait_recv()
     pack_far(0)
-    dy_gathers[1].step(9)
     partial(0, 3)
-    u_gather.near(1)
-    u_gather.far(0)
-    g_gather.other(1)
+    g_gather.far(0)
+    x_gather.step(0)
+    x_gather.step(1)
     across(0, 1).wait_recv()
     across(0, 2).wait_recv()
     pack_near(0)
+    x_gather.step(2)
+    dy_gathers[1].step(8)
+    dy_gathers[1].step(9)
+    for offset in (0, 1, -1, 2):
+        g_gather.from_sibling(0, offset)
+    activation(0)
+    g_gather.finish(0)
     dy_gathers[1].step(10)
     partial(1, 0)
     partial(1, 1)
-    u_gather.other(1)
-    for offset in (0, 1, -1, 2):
-        g_gather.from_sibling(0, offset)
-        u_gather.from_sibling(0, offset)
-    activation(0)
-    g_gather.finish(0)
-    u_gather.finish(0)
+    partial(1, 2)
+    partial(1, 3)
     across(1, 0).wait_recv()
     pack_far(1)
-    x_gather.step(0)
-    x_gather.step(1)
     g_gather.far(1)
-    partial(1, 2)
-    partial(1, 3)
-    x_gather.step(2)
     pack_sum(0)
+    x_gather.step(3)
+    x_gather.step(4)
     across(1, 1).wait_recv()
     across(1, 2).wait_recv()
     pack_near(1)
-    u_gather.far(1)
     for offset in (0, 1, -1, 2):
         g_gather.from_sibling(1, offset)
-        u_gather.from_sibling(1, offset)
-    x_gather.step(3)
-    x_gather.step(4)
     activation(1)
     g_gather.finish(1)
-    u_gather.finish(1)
-    down_tile(1)
+    down_tile(2)
     x_gather.step(5)
     down_tile(0)
     pack_sum(1)
-    down_tile(3)
+    down_tile(1)
+    x_gather.step(6)
     across(0, 3).wait_recv()
     finish_hidden(0)
-    down_tile(2)
+    x_gather.step(7)
+    down_tile(3)
+    x_gather.step(8)
     h_gather.from_sibling(0, 0)
     group_partial(0, 0)
-    x_gather.step(6)
-    x_gather.step(7)
-    x_gather.step(8)
     x_gather.step(9)
+    x_gather.step(10)
     across(1, 3).wait_recv()
     finish_hidden(1)
     for p in range(2):
@@ -538,18 +516,18 @@
     h_gather.near(0)
     group_second(0, 0)
     h_gather.other(0)
-    x_gather.step(10)
     h_gather.from_sibling(0, 1)
     group_partial(0, 1)
     h_gather.near(1)
     h_gather.from_sibling(0, -1)
     group_partial(0, 2)
     h_gather.other(1)
+    group_last(0, 0)
     group_second(1, 0)
-    group_last(0, 0)
     h_gather.from_sibling(1, 1)
     group_partial(1, 1)
     h_gather.far(0)
+    group_second(0, 1)
     h_gather.from_sibling(1, -1)
     group_partial(1, 2)
     h_gather.far(1)
@@ -558,35 +536,25 @@
     h_gather.from_sibling(1, 2)
     group_partial(1, 3)
     group_second(1, 1)
+    pair_tile(0)
+    group_second(1, 2)
+    pair_tile(2)
+    group_second(0, 3)
     group_second(0, 2)
-    group_second(0, 1)
-    gate_tile(3)
-    group_second(1, 2)
-    group_last(1, 0)
-    up_tile(3)
-    up_tile(0)
-    group_second(0, 3)
-    up_tile(1)
-    up_tile(2)
+    pair_tile(1)
     group_second(1, 3)
     group_last(1, 1)
-    gate_tile(0)
+    group_last(0, 1)
+    group_last(1, 0)
+    pair_tile(3)
+    group_last(1, 2)
     group_last(0, 2)
-    group_last(0, 1)
-    group_last(1, 2)
-    gate_tile(1)
     group_last(0, 3)
-    gate_tile(2)
     group_last(1, 3)
     for p in range(2):
         for n in range(6):
             ring_copy(p, n).wait_send()
 
-    gi_copy = pltpu.make_async_copy(gi, gi_out, lsem.at[0])
-    gi_copy.start()
-    for copy in outs[-4:]:
-        copy.wait()
-    gi_copy.wait()
     dy_gathers[0].finish()
     dy_gathers[1].finish()
     x_gather.finish()
@@ -602,26 +570,18 @@
     lax.fori_loop(0, 16, drain, 0)
 
 
-def hand_over(*refs):
-    sources, targets, held, come, gone = refs[:4], refs[4:8], refs[8:12], refs[12], refs[13]
-    parts = []
-    for source, target, hold in zip(sources, targets, held, strict=True):
-        rows = source.shape[0] // 4
-        for part in range(4):
-            here, n = pl.ds(part * rows, rows), len(parts)
-            parts.append(
-                (
-                    pltpu.make_async_copy(source.at[here], hold.at[here], come.at[n]),
-                    pltpu.make_async_copy(hold.at[here], target.at[here], gone.at[n]),
-                )
-            )
-    for first, _ in parts:
-        first.start()
-    for first, second in parts:
-        first.wait()
-        second.start()
-    for _, second in parts:
-        second.wait()
+def hand_over(gi, gw, gd, gi_out, gg_out, gu_out, gd_out, sems):
+    copies = [
+        (gw.at[:, pl.ds(0, 896)], gg_out),
+        (gw.at[:, pl.ds(896, 896)], gu_out),
+        (gd, gd_out),
+        (gi, gi_out),
+    ]
+    copies = [pltpu.make_async_copy(src, dst, sems.at[n]) for n, (src, dst) in enumerate(copies)]
+    for copy in copies:
+        copy.start()
+    for copy in copies:
+        copy.wait()
 
 
 def per_device(
@@ -629,6 +589,8 @@
 ):
     anywhere = pl.BlockSpec(memory_space=pl.ANY)
     scalars = pl.BlockSpec(memory_space=pltpu.SMEM)
+    vmem = pl.BlockSpec(memory_space=pltpu.VMEM)
+    held = [pltpu.VMEM((128, 1024), BF), pltpu.VMEM((1024, 1792), BF), pltpu.VMEM((896, 1024), BF)]
     dma = pltpu.SemaphoreType.DMA
     flops = 2 * 2048 * 1024 * 896 * 6
     shapes = [
@@ -641,19 +603,15 @@
     up_parts = up_pre.reshape(2, 4, 2, 16, 896)
     results = pl.pallas_call(
         kernel,
-        out_shape=shapes,
+        out_shape=held,
         in_specs=[anywhere] * 7 + [scalars] * 3,
-        out_specs=[anywhere] * 4,
+        out_specs=[vmem] * 3,
         scratch_shapes=[
             pltpu.VMEM((16, 128, 1024), BF),
             pltpu.VMEM((16, 128, 1024), BF),
-            pltpu.VMEM((16, 4, 2, 16, 896), BF),
-            pltpu.VMEM((16, 4, 2, 16, 896), BF),
+            pltpu.VMEM((16, 4, 2, 16, 1792), BF),
             pltpu.VMEM((8, 2, 2, 4, 16, 896), BF),
             pltpu.VMEM((16, 4, 2, 16, 896), BF),
-            pltpu.VMEM((1024, 896), BF),
-            pltpu.VMEM((1024, 896), BF),
-            pltpu.VMEM((896, 1024), BF),
             pltpu.VMEM((4, 4, 4, 32, 1024), F32),
             pltpu.VMEM((4, 4, 4, 16, 1024), F32),
             pltpu.VMEM((4, 2, 4, 32, 896), F32),
@@ -663,14 +621,11 @@
             pltpu.VMEM((16, 3, 4, 16, 512), BF),
             pltpu.VMEM((16, 3, 16, 512), BF),
             pltpu.VMEM((16, 3, 16, 512), BF),
-            pltpu.VMEM((128, 1024), BF),
-            pltpu.VMEM((4, 256, 1024), BF),
             dma((7,)),
-            dma((4,)),
             dma((3, 60)),
             dma((3, 4, 16)),
-            dma((3, 28)),
-            dma((3, 2, 2, 8)),
+            dma((2, 28)),
+            dma((2, 2, 2, 8)),
             dma((2, 4)),
             dma((2, 4)),
             dma((2, 6)),
@@ -679,18 +634,19 @@
             dma((16, 2, 3)),
         ],
         compiler_params=pltpu.CompilerParams(
-            collective_id=0, has_side_effects=True, vmem_limit_bytes=62 * 2**20
+            collective_id=0, has_side_effects=True, vmem_limit_bytes=52 * 2**20
         ),
         cost_estimate=pl.CostEstimate(flops=flops, bytes_accessed=18 * 2**20, transcendentals=4 * 2048 * 896),
     )(inputs, grad_out, gate_parts, up_parts, w_gate, w_up, w_down, mask_gate, mask_up, mask_down)
+    results = [pltpu.with_memory_space_constraint(result, pltpu.VMEM) for result in results]
     return pl.pallas_call(
         hand_over,
         out_shape=shapes,
-        in_specs=[anywhere] * 4,
+        in_specs=[vmem] * 3,
         out_specs=[anywhere] * 4,
-        scratch_shapes=[pltpu.VMEM(shape.shape, BF) for shape in shapes] + [dma((16,)), dma((16,))],
-        compiler_params=pltpu.CompilerParams(vmem_limit_bytes=62 * 2**20),
-        cost_estimate=pl.CostEstimate(flops=0, bytes_accessed=12 * 2**20, transcendentals=0),
+        scratch_shapes=[dma((4,))],
+        compiler_params=pltpu.CompilerParams(vmem_limit_bytes=2 * 2**20),
+        cost_estimate=pl.CostEstimate(flops=0, bytes_accessed=6 * 2**20, transcendentals=0),
     )(*results)
 
 

time: 105 us -> 98.4 us (0.937)
  Pallas kernels: 104 us -> 97.5 us
    pallas_call x2, Pallas kernels: 104 us -> 97.5 us  [the longest x1 94.9 us: per_device(): pl.pallas_call(kernel, out_shape=held, in_specs=[anywhere] * 7 + [scalars...]
where the time goes in v3:
time: 98.4 us; the launch traced here: 98.3 us
  Pallas kernels  97.5 us (99%)
    pallas_call x1, Pallas kernels, per_device(): pl.pallas_call(kernel, out_shape=held, in_specs=[anywhere] * 7 + [scalars...  94.9 us
    pallas_call x1, Pallas kernels, per_device(): pl.pallas_call(hand_over, out_shape=shapes, in_specs=[vmem] * 3, out_spec...  2.55 us

profile of v3, /device:TPU:1, one launch (start us, length us, event | category | flops | bytes accessed | tf_op | source)
XLA Modules:
  0.0 98.3 jit_solution(14188498307781476860)
XLA Ops:
  0.6 94.9 %shard_map.129 = (bf16[128,1024]{1,0:T(8,128)(2,1)S(1)}, bf16[1024,1792]{1,0:T(8,128)(2,1)S(1)}, bf16[896,1024]{1,0:T(8,128)(2,1)S(1)}) custom-call(bf16[128,1024]{1,0:T(8,128)(2,1)} %x_in.1, bf16[128,1024]{1,0:T(8,128)(2,1)} %dy_in.1, bf16[2,4,2,16,896]{4,3,2,1,0:T(8,128)(2,1)} %bitcast.2, bf16[2,4,2,16,896]{4,3,2,1,0:T(8,128)(2,1)} %bitcast.3, ...), custom_call_target="tpu_custom_call" | custom-call | flops 22548578304 | bytes 18874368 | tf_op jit(solution)/shard_map/pallas_call | solution.py:604
  95.6 2.6 %shard_map.130 = (bf16[128,1024]{1,0:T(8,128)(2,1)}, bf16[1024,896]{1,0:T(8,128)(2,1)}, bf16[1024,896]{1,0:T(8,128)(2,1)}, bf16[896,1024]{1,0:T(8,128)(2,1)}) custom-call(bf16[128,1024]{1,0:T(8,128)(2,1)S(1)} %get-tuple-element.7.gi, bf16[1024,1792]{1,0:T(8,128)(2,1)S(1)} %get-tuple-element.8.gw, bf16[896,1024]{1,0:T(8,128)(2,1)S(1)} %get-tuple-element.9.gd), custom_call_target="tpu_custom_call" | custom-call | bytes 6291456 | tf_op jit(solution)/shard_map/pallas_call | solution.py:642

commit v4 on v3

--- a/solution.py
+++ b/solution.py
@@ -34,8 +34,8 @@
 
 
 class ColGather:
-    def __init__(self, full, send, recv, at, rows):
-        self.full, self.send_sem, self.recv_sem = full, send, recv
+    def __init__(self, full, send, recv, last, at, rows):
+        self.full, self.send_sem, self.recv_sem, self.last_sem = full, send, recv, last
         self.at, self.rows = at, rows
         self.y, self.k, self.x, self.z = coords()
 
@@ -46,21 +46,20 @@
         late = lax.div(q, 2)
         return m4(self.x + a * (1 - late) + b * late) * 4 + m4(self.z + a * late + b * (1 - late))
 
-    def send(self, q, a, b, second, d, slot):
+    def send(self, q, a, b, second, d, last=False):
         c = self.index(q, a, b)
         late = lax.div(q, 2)
         along_z = late + second - 2 * late * second
         to = device(self.y, self.k, m4(self.x + d * (1 - along_z)), m4(self.z + d * along_z))
-        remote(
-            self.piece(q, c), self.piece(q, c), self.send_sem.at[q * 15 + slot], self.recv_sem.at[q, c], to
-        ).start()
+        recv = self.last_sem if last else self.recv_sem.at[q, c]
+        remote(self.piece(q, c), self.piece(q, c), self.send_sem, recv, to).start()
 
     def recv(self, q, a, b):
         c = self.index(q, a, b)
         remote(
             self.piece(q, c),
             self.piece(q, c),
-            self.send_sem.at[0],
+            self.send_sem,
             self.recv_sem.at[q, c],
             device(self.y, self.k, m4(self.x + 1), self.z),
         ).wait_recv()
@@ -74,65 +73,61 @@
 
     def start(self, second):
         def own(q, w):
-            self.send(q, 0, 0, 0, 1, 0)
-            self.send(q, 0, 0, 0, -1, 1)
+            self.send(q, 0, 0, 0, w)
+            self.send(q, 0, 0, 0, -w)
 
         def own_second(q, w):
-            self.send(q, 0, 0, 1, 1, 2)
-            self.send(q, 0, 0, 1, -1, 3)
+            self.onward(q, 0, w)
 
         self.each(own_second if second else own)
+
+    def onward(self, q, a, w):
+        self.send(q, a, 0, 1, w)
+        self.send(q, a, 0, 1, -w, last=True)
 
     def step(self, number):
         def first(q, w):
             self.recv(q, -w, 0)
-            self.send(q, -w, 0, 0, w, 4)
-            self.send(q, -w, 0, 1, 1, 5)
-            self.send(q, -w, 0, 1, -1, 6)
+            self.send(q, -w, 0, 0, w)
+            self.onward(q, -w, w)
 
         def second(q, w):
             self.recv(q, w, 0)
-            self.send(q, w, 0, 1, 1, 7)
-            self.send(q, w, 0, 1, -1, 8)
+            self.onward(q, w, w)
 
         def own_line(q, w):
             self.recv(q, 0, -w)
-            self.send(q, 0, -w, 1, w, 9)
+            self.send(q, 0, -w, 1, w, last=True)
 
         def far(q, w):
             self.recv(q, 2, 0)
-            self.send(q, 2, 0, 1, 1, 10)
-            self.send(q, 2, 0, 1, -1, 11)
+            self.onward(q, 2, w)
 
         def line(q, w):
             a = (-1, 1, 2)[number - 4]
             self.recv(q, a * w, -w)
-            self.send(q, a * w, -w, 1, w, 8 + number)
-
-        def last(q, w):
-            a = (0, -1, 1, 2)[number - 7]
-            self.recv(q, a * w, w)
-            self.recv(q, a * w, 2)
-
-        self.each((first, second, own_line, far, line, line, line, last, last, last, last)[number])
+            self.send(q, a * w, -w, 1, w, last=True)
+
+        if number < 7:
+            self.each((first, second, own_line, far, line, line, line)[number])
+        elif number == 10:
+            self.bytes_of(32).wait_recv()
+
+    def bytes_of(self, pieces):
+        view = self.full.at[pl.ds(0, pieces * self.rows // 128)]
+        to = device(self.y, self.k, m4(self.x + 1), self.z)
+        return remote(view, view, self.send_sem, self.last_sem, to)
 
     def finish(self):
-        def one(i, carry):
-            remote(
-                self.piece(0, 0),
-                self.piece(0, 0),
-                self.send_sem.at[i],
-                self.recv_sem.at[0, 0],
-                device(self.y, self.k, m4(self.x + 1), self.z),
-            ).wait_send()
-            return carry
-
-        lax.fori_loop(0, 60, one, 0)
+        view = self.full.at[pl.ds(0, 15), pl.ds(0, 4 * self.rows)]
+        to = device(self.y, self.k, m4(self.x + 1), self.z)
+        remote(view, view, self.send_sem, self.last_sem, to).wait_send()
 
 
 class RowGather:
-    def __init__(self, view, send, recv):
-        self.view, self.send_sem, self.recv_sem = view, send, recv
+    def __init__(self, view, both, sent, send, recv, cross_recv):
+        self.view, self.both, self.sent = view, both, sent
+        self.send_sem, self.recv_sem, self.cross_sem = send, recv, cross_recv
         self.y, self.k, self.x, self.z = coords()
 
     def row(self, dy, sibling=False):
@@ -141,58 +136,59 @@
     def sibling(self):
         return device(self.y, 1 - self.k, self.x, self.z)
 
-    def copy(self, p, h, r, slot, to):
+    def ring_copy(self, p, h, r, to):
         view = self.view(r, p, h)
-        return remote(view, view, self.send_sem.at[p * 14 + h * 7 + slot], self.recv_sem.at[p, h, r], to)
-
-    def ring(self, p, h, dy, d, slot):
-        to = device(m4(self.y + d), self.k, self.x, self.z)
-        self.copy(p, h, self.row(dy), slot, to).start()
-
-    def cross(self, p, h, dy, slot):
-        self.copy(p, h, self.row(dy), slot, self.sibling()).start()
-
-    def recv(self, p, h, dy, sibling=False):
-        self.copy(p, h, self.row(dy, sibling), 0, self.sibling()).wait_recv()
+        return remote(view, view, self.send_sem.at[p], self.recv_sem.at[p, h, r], to)
+
+    def ring(self, p, h, dy, d):
+        self.ring_copy(p, h, self.row(dy), device(m4(self.y + d), self.k, self.x, self.z)).start()
+
+    def cross(self, p, h, dy):
+        r = self.row(dy)
+        view = self.view(r, p, h)
+        remote(view, view, self.send_sem.at[p], self.cross_sem.at[p, r], self.sibling()).start()
+
+    def recv(self, p, h, dy):
+        self.ring_copy(p, h, self.row(dy), self.sibling()).wait_recv()
 
     def start(self, p, second):
-        self.ring(p, second, 0, 1, 0)
-        self.ring(p, 1 - second, 0, -1, 1)
-        self.cross(p, second, 0, 2)
+        self.ring(p, second, 0, 1)
+        self.ring(p, 1 - second, 0, -1)
+        self.cross(p, second, 0)
 
     def near(self, p):
         for h in (0, 1):
             w = 1 - 2 * h
             self.recv(p, h, -w)
-            self.ring(p, h, -w, w, 3)
-            self.cross(p, h, -w, 4)
+            self.ring(p, h, -w, w)
+            self.cross(p, h, -w)
 
     def other(self, p):
         for h in (0, 1):
             w = 1 - 2 * h
             self.recv(p, h, w)
-            self.cross(p, h, w, 5)
+            self.cross(p, h, w)
 
     def far(self, p):
         for h in (0, 1):
             self.recv(p, h, 2)
-            self.cross(p, h, 2, 6)
+            self.cross(p, h, 2)
 
     def from_sibling(self, p, dy):
-        for h in (0, 1):
-            self.recv(p, h, dy, True)
+        r = self.row(dy, True)
+        view = self.both(r, p)
+        remote(view, view, self.send_sem.at[p], self.cross_sem.at[p, r], self.sibling()).wait_recv()
 
     def finish(self, p):
-        for h in (0, 1):
-            for slot in range(7):
-                self.copy(p, h, 0, slot, self.sibling()).wait_send()
+        view = self.sent(p)
+        remote(view, view, self.send_sem.at[p], self.cross_sem.at[p, 0], self.sibling()).wait_send()
 
 
 def kernel(
-    x_in, dy_in, g_in, u_in, wg_in, wu_in, wd_in, mg, mu, md,
+    x_in, dy_in, g_in, u_in, wg_in, wu_in, wd_in, mg_in, mu_in, md_in,
     gi, gw, gd,
     dy, xx, gu, hd, act, hp, pa, rb, ys, yr, s1, r1, s2, r2,
-    lsem, col_s, col_r, row_s, row_r, sib_s, sib_r, ring_s, ring_r, gs, gr,
+    mg, mu, md, lsem, col_s, col_r, col_l, row_s, row_r, row_c, sib_s, sib_r, ring_s, ring_r, gs, gr,
 ):
     y, k, x, z = coords()
     me_col, me_row = x * 4 + z, y * 2 + k
@@ -208,6 +204,9 @@
         pltpu.make_async_copy(x_in, xx.at[me_col], lsem.at[4]),
         pltpu.make_async_copy(wg_in, gw.at[:, left_half], lsem.at[5]),
         pltpu.make_async_copy(wu_in, gw.at[:, right_half], lsem.at[6]),
+        pltpu.make_async_copy(md_in, md, lsem.at[7]),
+        pltpu.make_async_copy(mg_in, mg, lsem.at[8]),
+        pltpu.make_async_copy(mu_in, mu, lsem.at[9]),
     ]
     for copy in local:
         copy.start()
@@ -227,10 +226,24 @@
         pl.semaphore_signal(barrier, inc=1, device_id=to, device_id_type=MESH)
     pl.semaphore_wait(barrier, 9)
 
-    dy_gathers = [ColGather(dy, col_s.at[p], col_r.at[p], 16 * p, 16) for p in range(2)]
-    x_gather = ColGather(xx, col_s.at[2], col_r.at[2], 0, 32)
-    g_gather = RowGather(lambda r, p, h: gu.at[2 * r + h, :, p], row_s.at[0], row_r.at[0])
-    h_gather = RowGather(lambda r, p, h: hd.at[r, p, h], row_s.at[1], row_r.at[1])
+    dy_gathers = [ColGather(dy, col_s.at[p], col_r.at[p], col_l.at[p], 16 * p, 16) for p in range(2)]
+    x_gather = ColGather(xx, col_s.at[2], col_r.at[2], col_l.at[2], 0, 32)
+    g_gather = RowGather(
+        lambda r, p, h: gu.at[2 * r + h, :, p],
+        lambda r, p: gu.at[pl.ds(2 * r, 2), :, p],
+        lambda p: gu.at[pl.ds(0, 14), :, p],
+        row_s.at[0],
+        row_r.at[0],
+        row_c.at[0],
+    )
+    h_gather = RowGather(
+        lambda r, p, h: hd.at[r, p, h],
+        lambda r, p: hd.at[r, p],
+        lambda p: hd.at[pl.ds(0, 7), p],
+        row_s.at[1],
+        row_r.at[1],
+        row_c.at[1],
+    )
 
     def apply_mask(w, mask, rows, columns, first=0):
         def line(i, carry):
@@ -267,7 +280,10 @@
 
     def ring_copy(p, n):
         to = up_y if n % 2 == 0 else down_y
-        return remote(ys.at[p, n], yr.at[p, n], ring_s.at[p, n], ring_r.at[p, n], to)
+        return remote(ys.at[p, n], yr.at[p, n], ring_s.at[p], ring_r.at[p, n], to)
+
+    def ring_sent(p):
+        remote(ys.at[p], yr.at[p], ring_s.at[p], ring_r.at[p, 0], up_y).wait_send()
 
     def pack(p, n, slot, h, with_recv=None):
         if with_recv is not None:
@@ -351,7 +367,12 @@
             to = device(y, k, m4(x + d), z)
         at = p * 8 + n * 2 + t
         src, dst = (s1, r1) if stage_at == 0 else (s2, r2)
-        return remote(src.at[at, i], dst.at[at, i], gs.at[at, stage_at, i], gr.at[at, stage_at, i], to)
+        return remote(src.at[at, i], dst.at[at, i], gs.at[stage_at], gr.at[p * 4 + n, stage_at], to)
+
+    def group_wait(p, n, stage_at):
+        both = pl.ds(p * 8 + n * 2, 2)
+        src, dst = (s1, r1) if stage_at == 0 else (s2, r2)
+        remote(src.at[both], dst.at[both], gs.at[stage_at], gr.at[p * 4 + n, stage_at], sibling).wait_recv()
 
     def columns(t):
         return pl.ds(t * 512, 512)
@@ -393,9 +414,7 @@
         return own
 
     def group_second(p, n):
-        for t in range(2):
-            for i in range(3):
-                group_copy(p, n, t, 0, i).wait_recv()
+        group_wait(p, n, 0)
         for i, d in enumerate(offsets):
             for t in range(2):
                 s2[p * 8 + n * 2 + t, i] = line_total(p, n, t, d).astype(BF)
@@ -404,10 +423,10 @@
     def group_last(p, n):
         j = m4(y + GROUPS[n])
         rows = pl.ds(pl.multiple_of(j * 32 + p * 16, 16), 16)
+        group_wait(p, n, 1)
         for t in range(2):
             value = line_total(p, n, t, 0)
             for i in range(3):
-                group_copy(p, n, t, 1, i).wait_recv()
                 value = value + r2[p * 8 + n * 2 + t, i].astype(F32)
             gi[rows, columns(t)] = value.astype(BF)
 
@@ -432,10 +451,13 @@
     dy_gathers[0].step(4)
     dy_gathers[0].step(5)
     local[3].wait()
+    local[7].wait()
     apply_mask(gd, md, 7, 8)
     local[5].wait()
+    local[8].wait()
     apply_mask(gw, mg, 8, 7)
     local[6].wait()
+    local[9].wait()
     apply_mask(gw, mu, 8, 7, 896)
     dy_gathers[1].step(0)
     dy_gathers[1].step(1)
@@ -551,9 +573,8 @@
     group_last(0, 2)
     group_last(0, 3)
     group_last(1, 3)
-    for p in range(2):
-        for n in range(6):
-            ring_copy(p, n).wait_send()
+    ring_sent(0)
+    ring_sent(1)
 
     dy_gathers[0].finish()
     dy_gathers[1].finish()
@@ -561,13 +582,8 @@
     h_gather.finish(0)
     h_gather.finish(1)
 
-    def drain(at, carry):
-        for kind in range(3):
-            remote(s1.at[0, 0], r1.at[0, 0], gs.at[at, 0, kind], gr.at[0, 0, 0], sibling).wait_send()
-            remote(s2.at[0, 0], r2.at[0, 0], gs.at[at, 1, kind], gr.at[0, 1, 0], sibling).wait_send()
-        return carry
-
-    lax.fori_loop(0, 16, drain, 0)
+    remote(s1, r1, gs.at[0], gr.at[0, 0], sibling).wait_send()
+    remote(s2, r2, gs.at[1], gr.at[0, 1], sibling).wait_send()
 
 
 def hand_over(gi, gw, gd, gi_out, gg_out, gu_out, gd_out, sems):
@@ -588,7 +604,6 @@
     inputs, grad_out, gate_pre, up_pre, w_gate, w_up, w_down, mask_gate, mask_up, mask_down
 ):
     anywhere = pl.BlockSpec(memory_space=pl.ANY)
-    scalars = pl.BlockSpec(memory_space=pltpu.SMEM)
     vmem = pl.BlockSpec(memory_space=pltpu.VMEM)
     held = [pltpu.VMEM((128, 1024), BF), pltpu.VMEM((1024, 1792), BF), pltpu.VMEM((896, 1024), BF)]
     dma = pltpu.SemaphoreType.DMA
@@ -604,7 +619,7 @@
     results = pl.pallas_call(
         kernel,
         out_shape=held,
-        in_specs=[anywhere] * 7 + [scalars] * 3,
+        in_specs=[anywhere] * 10,
         out_specs=[vmem] * 3,
         scratch_shapes=[
             pltpu.VMEM((16, 128, 1024), BF),
@@ -621,17 +636,22 @@
             pltpu.VMEM((16, 3, 4, 16, 512), BF),
             pltpu.VMEM((16, 3, 16, 512), BF),
             pltpu.VMEM((16, 3, 16, 512), BF),
-            dma((7,)),
-            dma((3, 60)),
+            pltpu.SMEM((8, 7), jnp.int32),
+            pltpu.SMEM((8, 7), jnp.int32),
+            pltpu.SMEM((7, 8), jnp.int32),
+            dma((10,)),
+            dma((3,)),
             dma((3, 4, 16)),
-            dma((2, 28)),
+            dma((3,)),
+            dma((2, 2)),
             dma((2, 2, 2, 8)),
+            dma((2, 2, 8)),
             dma((2, 4)),
             dma((2, 4)),
+            dma((2,)),
             dma((2, 6)),
-            dma((2, 6)),
-            dma((16, 2, 3)),
-            dma((16, 2, 3)),
+            dma((2,)),
+            dma((8, 2)),
         ],
         compiler_params=pltpu.CompilerParams(
             collective_id=0, has_side_effects=True, vmem_limit_bytes=52 * 2**20

time: 98.4 us -> 92.5 us (0.940)
  Pallas kernels: 97.5 us -> 91.6 us
    pallas_call x1, Pallas kernels: 94.9 us -> 89 us  [per_device(): pl.pallas_call(kernel, out_shape=held, in_specs=[anywhere] * 10, out_spec...]
where the time goes in v4:
time: 92.5 us; the launch traced here: 92.4 us
  Pallas kernels  91.6 us (99%)
    pallas_call x1, Pallas kernels, per_device(): pl.pallas_call(kernel, out_shape=held, in_specs=[anywhere] * 10, out_spec...  89 us
    pallas_call x1, Pallas kernels, per_device(): pl.pallas_call(hand_over, out_shape=shapes, in_specs=[vmem] * 3, out_spec...  2.55 us

profile of v4, /device:TPU:1, one launch (start us, length us, event | category | flops | bytes accessed | tf_op | source)
XLA Modules:
  0.0 92.4 jit_solution(6032761296851433031)
XLA Ops:
  0.6 89.0 %shard_map.129 = (bf16[128,1024]{1,0:T(8,128)(2,1)S(1)}, bf16[1024,1792]{1,0:T(8,128)(2,1)S(1)}, bf16[896,1024]{1,0:T(8,128)(2,1)S(1)}) custom-call(bf16[128,1024]{1,0:T(8,128)(2,1)} %x_in.1, bf16[128,1024]{1,0:T(8,128)(2,1)} %dy_in.1, bf16[2,4,2,16,896]{4,3,2,1,0:T(8,128)(2,1)} %bitcast.2, bf16[2,4,2,16,896]{4,3,2,1,0:T(8,128)(2,1)} %bitcast.3, ...), custom_call_target="tpu_custom_call" | custom-call | flops 22548578304 | bytes 18874368 | tf_op jit(solution)/shard_map/pallas_call | solution.py:619
  89.7 2.6 %shard_map.130 = (bf16[128,1024]{1,0:T(8,128)(2,1)}, bf16[1024,896]{1,0:T(8,128)(2,1)}, bf16[1024,896]{1,0:T(8,128)(2,1)}, bf16[896,1024]{1,0:T(8,128)(2,1)}) custom-call(bf16[128,1024]{1,0:T(8,128)(2,1)S(1)} %get-tuple-element.7.gi, bf16[1024,1792]{1,0:T(8,128)(2,1)S(1)} %get-tuple-element.8.gw, bf16[896,1024]{1,0:T(8,128)(2,1)S(1)} %get-tuple-element.9.gd), custom_call_target="tpu_custom_call" | custom-call | bytes 6291456 | tf_op jit(solution)/shard_map/pallas_call | solution.py:662
